TPU v7x, 512 devices: a whole 4x8x8 slice. The times are simulated.
512 devices in a mesh: band: 16 (over y, core), tan: 32 (over x, z).
Axes of the slice: x: 4, y: 8, z: 8, core: 2. Of those that a mesh axis runs over, the one named last changes fastest.
Arguments:
- grid: bfloat16 [128, 2, 1280, 2560], P('tan', None, 'band'), may hold values from -6 to 6
- trunc: int32 [1280], P('band'), may hold values from 0 to 1279
- wlist: int32 [16], replicated, may hold values from 0 to 639, as said below
- leg_even: bfloat16 [16, 640, 641], P('band'), may hold values from -0.25 to 0.25
- leg_odd: bfloat16 [16, 640, 640], P('band'), may hold values from -0.25 to 0.25
Outputs:
- even_coeffs: float32 [16, 128, 2, 2, 641], P('band', 'tan')
- odd_coeffs: float32 [16, 128, 2, 2, 640], P('band', 'tan')
- inner: float32 [128, 128], P(None, 'tan')
Inputs may be any that keep to these rules, and one draw needn't show every extreme that they name: Distinct values; band index b owns wavenumbers wlist[b] and 1279 - wlist[b]; wavenumbers 0 and 639 are always owned.
All inputs are finite; a program needn't handle non-finite values.
Results may differ from a plain program's by a relative error of at most 0.0051.
Values may be sent and summed in bfloat16 or wider, within the bound.
No kernel may reach another device: no remote copies, remote signals or barrier semaphores. Data moves between devices by JAX's collectives and lax.ppermute only.
A program may use at most 64 MiB of HBM per device.

v0:
```python
import math

import jax
import jax.numpy as jnp
from jax import lax
from jax.sharding import PartitionSpec as P


def fourier_table(mvals, lon_count):
    longitude = jnp.arange(lon_count, dtype=jnp.int32)
    phase = longitude[:, None, None] * mvals[None, :, :] % lon_count
    angle = phase.astype(jnp.float32) * (2.0 * math.pi / lon_count)
    scaling = 1.0 / math.sqrt(lon_count)
    table = jnp.stack([jnp.cos(angle) * scaling, -jnp.sin(angle) * scaling], axis=3)
    return table.astype(jnp.bfloat16)


def on_device(grid, trunc, wlist, leg_even, leg_odd):
    band_count = lax.axis_size("band")
    band_index = lax.axis_index("band")
    vectors, field_count, lat_count, lon_count = grid.shape
    total_lat = lat_count * band_count
    hemisphere = total_lat // 2
    mvals = jnp.stack([wlist, total_lat - 1 - wlist], axis=1)
    table = fourier_table(mvals, lon_count)
    spectra = jnp.einsum("vfjk,kbpr->bjprvf", grid, table, preferred_element_type=jnp.float32)
    keeper = (mvals[:, None, :] <= trunc[None, :, None]).astype(jnp.float32)
    lat_rows = (spectra * keeper[:, :, :, None, None, None]).astype(jnp.bfloat16)
    row_width = 4 * vectors * field_count
    lat_rows = lat_rows.reshape(band_count, lat_count, row_width)
    received = lax.all_to_all(lat_rows, "band", split_axis=0, concat_axis=1, tiled=True)
    received = received.reshape(total_lat, 2, 2, vectors, field_count)
    northern = received[:hemisphere].astype(jnp.float32)
    southern = received[hemisphere:][::-1].astype(jnp.float32)
    sym_rows = (northern + southern).astype(jnp.bfloat16)
    anti_rows = (northern - southern).astype(jnp.bfloat16)
    even_all = jnp.einsum(
        "jprvf,jc->pvfrc", sym_rows, leg_even[0], preferred_element_type=jnp.float32
    )
    odd_all = jnp.einsum(
        "jprvf,jc->pvfrc", anti_rows, leg_odd[0], preferred_element_type=jnp.float32
    )
    own_wave = wlist[band_index]
    even_cols = jnp.arange(leg_even.shape[2], dtype=jnp.int32)
    odd_cols = jnp.arange(leg_odd.shape[2], dtype=jnp.int32)
    even_coeffs = jnp.where(even_cols < (total_lat + 1 - own_wave) // 2, even_all[0], even_all[1])
    odd_coeffs = jnp.where(odd_cols < (total_lat - own_wave) // 2, odd_all[0], odd_all[1])
    packed = jnp.concatenate([even_coeffs, odd_coeffs], axis=-1).astype(jnp.bfloat16)
    packed = packed.reshape(vectors, -1)
    partial_sums = jnp.einsum(
        "ak,ck->ac",
        lax.all_gather(packed, "tan", axis=0, tiled=True),
        packed,
        preferred_element_type=jnp.float32,
    )
    summed = lax.psum(partial_sums, "band")
    inner = summed / (band_count * 4.0 * (total_lat + 1))
    return (even_coeffs[None], odd_coeffs[None], inner)


def solution(mesh):
    return jax.shard_map(
        on_device,
        mesh=mesh,
        in_specs=(
            P("tan", None, "band", None),
            P("band"),
            P(),
            P("band", None, None),
            P("band", None, None),
        ),
        out_specs=(
            P("band", "tan", None, None, None),
            P("band", "tan", None, None, None),
            P(None, "tan"),
        ),
        check_vma=False,
    )
```

profile of v0, /device:TPU:1, one launch (start us, length us, event | category | flops | bytes accessed | tf_op | source)
XLA Modules:
  0.0 155.2 jit_solution(6848300184761756585)
XLA Ops:
  7.2 0.8 subtract_bitcast_fusion
  8.0 0.8 pad_add_fusion
  8.8 1.5 multiply_convert_fusion.1
  10.4 0.7 compare_convert_fusion
  11.1 1.4 fusion.8
  12.5 0.7 copy.25
  13.2 10.2 %all-to-all-start = ((bf16[16,80,32]{1,2,0:T(8,128)(2,1)}), bf16[16,80,32]{1,2,0:T(8,128)(2,1)S(1)}, u32[]{:S(2)}, u32[]{:S(2)}) async-start(bf16[16,80,32]{1,2,0:T(8,128)(2,1)} %copy.25), calls=%async_computation | async-start | bytes 262144 | tf_op jit(solution)/shard_map/all_to_all | solution.py:31
  23.5 0.6 dynamic_slice.3
  24.7 0.6 iota_compare_fusion.1
  26.0 0.6 iota_compare_fusion
  26.5 6.1 %all-to-all-done = bf16[16,80,32]{1,2,0:T(8,128)(2,1)S(1)} async-done(((bf16[16,80,32]{1,2,0:T(8,128)(2,1)}), bf16[16,80,32]{1,2,0:T(8,128)(2,1)S(1)}, u32[]{:S(2)}, u32[]{:S(2)}) %all-to-all-start) | async-done | bytes 81952 | tf_op jit(solution)/shard_map/all_to_all | solution.py:31
  33.1 0.5 rev.3
  33.7 0.6 copy-done.1
  34.3 1.4 convolution_bitcast_fusion.1
  35.7 1.6 %convolution_bitcast_fusion = f32[2,4,2,2,641]{4,1,2,3,0:T(4,128)S(1)} fusion(bf16[1,640,641]{1,2,0:T(8,128)(2,1)} %param.8, bf16[640,2,2,4,2]{0,3,4,2,1:T(4,128)(2,1)} %copy-done.1, f32[640,2,2,4,2]{0,4,3,2,1:T(2,128)S(1)} %reshape.78), kind=kOutput, calls=%fused_computation.5 | convolution fusion | flops 26316800 | bytes 1025408 | tf_op jit(solution)/shard_map/jprvf,jc->pvfrc/dot_general | solution.py:37
  37.5 0.7 reshape.79
  38.2 0.7 convert_element_type.53
  39.0 0.6 copy.34
  39.6 0.6 copy.33
  40.3 74.5 %all-gather.3.cloned.1.call-done = bf16[32,4,5124]{2,1,0:T(4,128)(2,1)} async-done(((bf16[1,4,5124]{2,1,0:T(4,128)(2,1)}), bf16[32,4,5124]{2,1,0:T(4,128)(2,1)}) %all-gather.3.cloned.1.call-update) | async-done | bytes 1311760 | tf_op jit(solution)/shard_map/all_gather | solution.py:52
  114.7 3.3 %reshape.80 = bf16[128,5124]{1,0:T(8,128)(2,1)} reshape(bf16[32,4,5124]{2,1,0:T(4,128)(2,1)} %all-gather.3.cloned.1.call-done) | data formatting | bytes 2623488
  118.1 1.7 %fusion.27 = f32[128,4]{0,1:T(4,128)S(1)} fusion(bf16[128,5124]{1,0:T(8,128)(2,1)} %reshape.80, bf16[4,5124]{1,0:T(4,128)(2,1)S(1)} %copy-done.2), kind=kOutput, calls=%fused_computation.40 | convolution fusion | flops 5246976 | bytes 1354784 | tf_op jit(solution)/shard_map/ak,ck->ac/dot_general | solution.py:50
  119.8 28.0 %psum.7 = f32[128,4]{0,1:T(4,128)S(1)} all-reduce(f32[128,4]{0,1:T(4,128)S(1)} %fusion.27), channel_id=1, replica_groups=mesh['band'=16,'tan'=32] {'band'}, use_global_device_ids=true, to_apply=%region_0.1 | all-reduce | flops 512 | bytes 4096 | tf_op jit(solution)/shard_map/psum | solution.py:56
  147.8 0.6 broadcast_multiply_fusion
  (25 shorter events, 0.7 us)
Async XLA Ops:
  7.2 3.9 %copy-start = (bf16[4,2,80,2560]{3,2,1,0:T(8,128)(2,1)S(1)}, bf16[4,2,80,2560]{3,2,1,0:T(8,128)(2,1)}, u32[]{:S(2)}) copy-start(bf16[4,2,80,2560]{3,2,1,0:T(8,128)(2,1)} %param.5) | copy-start | bytes 9830404
  11.1 12.4 %copy-start.5 = (s32[16]{0:T(128)S(1)}, s32[16]{0:T(128)}, u32[]{:S(2)}) copy-start(s32[16]{0:T(128)} %param.7) | copy-start | bytes 196
  13.2 19.4 %all-to-all-start = ((bf16[16,80,32]{1,2,0:T(8,128)(2,1)}), bf16[16,80,32]{1,2,0:T(8,128)(2,1)S(1)}, u32[]{:S(2)}, u32[]{:S(2)}) async-start(bf16[16,80,32]{1,2,0:T(8,128)(2,1)} %copy.25), calls=%async_computation | async-start | bytes 262144 | tf_op jit(solution)/shard_map/all_to_all | solution.py:31
  23.4 91.3 %all-gather.3.cloned.1.call-start = ((), (), s32[]{:S(2)}) async-start(), calls=%async_computation.1 | async-start | bytes 1385472 | tf_op jit(solution)/shard_map/all_gather | solution.py:52
  32.9 4.3 %copy-start.4 = (pred[640]{0:T(1024)(128)(4,1)S(1)}, pred[640]{0:T(1024)(128)(4,1)}, u32[]{:S(2)}) copy-start(pred[640]{0:T(1024)(128)(4,1)} %iota_compare_fusion) | copy-start | bytes 1924
  32.9 4.4 %copy-start.3 = (pred[641]{0:T(1024)(128)(4,1)S(1)}, pred[641]{0:T(1024)(128)(4,1)}, u32[]{:S(2)}) copy-start(pred[641]{0:T(1024)(128)(4,1)} %iota_compare_fusion.1) | copy-start | bytes 1927
  33.7 0.6 copy-start.1
  40.3 77.8 %copy-start.2 = (bf16[4,5124]{1,0:T(4,128)(2,1)S(1)}, bf16[4,5124]{1,0:T(4,128)(2,1)}, u32[]{:S(2)}) copy-start(bf16[4,5124]{1,0:T(4,128)(2,1)} %convert_element_type.53) | copy-start | bytes 122980
Sparse Core Ops, SparseCore 0:
  38.3 76.3 all-gather.2
where the time goes:
time: 156 us; the launch traced here: 155 us
  waiting for transfers between devices  80.6 us (52%)
  blocking collectives  28 us (18%)
  between operations  15.5 us (10%)
  starting transfers between devices  10.2 us (7%)
  local copies, waits for them, and re-layouts  9.01 us (6%)
  matrix products  6.15 us (4%)
  other arithmetic  5.79 us (4%)
    all_gather x1, waiting for transfers between devices, on_device(): lax.all_gather(packed, 'tan', axis=0, tiled=True)  74.5 us
    psum x1, blocking collectives, on_device(): summed = lax.psum(partial_sums, 'band')  28 us
    all_to_all x1, starting transfers between devices, on_device(): lax.all_to_all(lat_rows, 'band', split_axis=0, concat_axis=1, tiled=True)  10.2 us
    all_to_all x1, waiting for transfers between devices, on_device(): lax.all_to_all(lat_rows, 'band', split_axis=0, concat_axis=1, tiled=True)  6.09 us
    unnamed x16, local copies, waits for them, and re-layouts  6 us
  transfers between devices with their start and end apart: 2, of which 2 were waited for; matrix products, arithmetic and copies ran while one was open for 2% of the time, Pallas kernels for 0%

commit v1 on v0

v1 whole, which is shorter than its diff:
```python
import math

import jax
import jax.numpy as jnp
from jax import lax
from jax.experimental import pallas as pl
from jax.experimental.pallas import tpu as pltpu
from jax.sharding import PartitionSpec as P

F32 = jnp.float32
BF16 = jnp.bfloat16
NT = (((1,), (1,)), ((), ()))
NN = (((1,), (0,)), ((), ()))


def fourier_kernel(wlist_ref, trunc_ref, grid_ref, out_ref, table, rows):
    vectors, fields, lats, lons = grid_ref.shape
    bands = wlist_ref.shape[0]
    total_lat = lats * bands
    members = 2 * bands
    row = lax.broadcasted_iota(jnp.int32, (members, 128), 0)
    lane = lax.broadcasted_iota(jnp.int32, (members, 128), 1)
    mvals = jnp.zeros((members, 128), jnp.int32)
    for b in range(bands):
        wave = wlist_ref[b]
        mvals = jnp.where(row == b, wave, mvals)
        mvals = jnp.where(row == bands + b, total_lat - 1 - wave, mvals)
    unit = 2.0 * math.pi / lons
    scaling = 1.0 / math.sqrt(lons)
    chunks = lons // 128
    fine = (mvals * lane % lons).astype(F32) * unit
    coarse = (mvals * lane % chunks).astype(F32) * (128.0 * unit)
    fine_cos, fine_sin = jnp.cos(fine), jnp.sin(fine)
    coarse_cos, coarse_sin = jnp.cos(coarse) * scaling, jnp.sin(coarse) * scaling
    for i in range(chunks):
        cc, cs = coarse_cos[:, i : i + 1], coarse_sin[:, i : i + 1]
        table[:members, 128 * i : 128 * (i + 1)] = (cc * fine_cos - cs * fine_sin).astype(BF16)
        table[members:, 128 * i : 128 * (i + 1)] = (-(cs * fine_cos + cc * fine_sin)).astype(BF16)
    keep = mvals[:, :lats] <= trunc_ref[...]
    keep = jnp.concatenate([keep, keep], axis=0)
    depth = 4 * vectors * fields
    for v in range(vectors):
        for f in range(fields):
            spectra = lax.dot_general(table[...], grid_ref[v, f], NT, preferred_element_type=F32)
            spectra = jnp.where(keep, spectra, 0.0)
            spectra = jnp.pad(spectra, ((0, 0), (0, 128 - lats)))
            for r in range(2):
                for p in range(2):
                    place = ((p * fields + f) * 2 + r) * vectors + v
                    start = (r * 2 + p) * bands
                    rows[pl.ds(place, bands, stride=depth), :] = spectra[start : start + bands]
    out_ref[...] = rows[...].astype(BF16).reshape(out_ref.shape)


def legendre_kernel(wlist_ref, rows_ref, even_t_ref, odd_ref, even_ref, odd_out_ref, send_ref, fold):
    bands, depth, _ = rows_ref.shape
    half_bands = bands // 2
    hemisphere = odd_ref.shape[1]
    lats = hemisphere // half_bands
    total_lat = 2 * hemisphere
    fields, vectors = even_ref.shape[2], even_ref.shape[1]
    own = wlist_ref[lax.axis_index("band")]
    ri = lax.broadcasted_iota(jnp.int32, (128, 128), 0)
    ci = lax.broadcasted_iota(jnp.int32, (128, 128), 1)
    mirror = jnp.where(ri + ci == lats - 1, 1.0, 0.0).astype(BF16)
    south = rows_ref[half_bands:].reshape(half_bands * depth, 128)
    south = lax.dot_general(south, mirror, NN, preferred_element_type=F32)
    for b in range(half_bands):
        north_b = rows_ref[b].astype(F32)
        s = half_bands - 1 - b
        south_b = south[s * depth : (s + 1) * depth]
        fold[0, :, lats * b : lats * (b + 1)] = (north_b + south_b)[:, :lats]
        fold[1, :, lats * b : lats * (b + 1)] = (north_b - south_b)[:, :lats]
    sym, anti = fold[0].astype(BF16), fold[1].astype(BF16)
    even_all = lax.dot_general(sym, even_t_ref[0], NT, preferred_element_type=F32)
    odd_all = lax.dot_general(anti, odd_ref[0], NN, preferred_element_type=F32)
    half = depth // 2
    even_col = lax.broadcasted_iota(jnp.int32, (half, hemisphere + 1), 1)
    odd_col = lax.broadcasted_iota(jnp.int32, (half, hemisphere), 1)
    even = jnp.where(even_col < (total_lat + 1 - own) // 2, even_all[:half], even_all[half:])
    odd = jnp.where(odd_col < (total_lat - own) // 2, odd_all[:half], odd_all[half:])
    parts = fields * 2
    for fr in range(parts):
        for v in range(vectors):
            f, r, place = fr // 2, fr % 2, fr * vectors + v
            even_ref[0, v, f, r : r + 1, :] = even[place : place + 1]
            odd_out_ref[0, v, f, r : r + 1, :] = odd[place : place + 1]
    tiles = hemisphere // 128
    first = lax.broadcasted_iota(jnp.int32, (8, 128), 0) < vectors
    corner = (lax.broadcasted_iota(jnp.int32, (8, 128), 1) == 0) & first
    for fr in range(parts):
        base = fr // 2 * 8
        for i in range(tiles):
            ev = even[base : base + 8, 128 * i : 128 * (i + 1)]
            od = odd[base : base + 8, 128 * i : 128 * (i + 1)]
            if fr % 2 == 0:
                tile = jnp.where(first, ev, pltpu.roll(od, 4, 0))
            else:
                tile = jnp.where(first, pltpu.roll(ev, 4, 0), od)
            send_ref[fr * tiles + i] = tile.astype(BF16)
        last = jnp.broadcast_to(even[base : base + 8, hemisphere : hemisphere + 1], (8, 128))
        if fr % 2 == 1:
            last = pltpu.roll(last, 4, 0)
        send_ref[parts * tiles + fr] = jnp.where(corner, last, 0.0).astype(BF16)
    for t in range(parts * (tiles + 1), send_ref.shape[0]):
        send_ref[t] = jnp.zeros((8, 128), BF16)


def gram_kernel(tiles_ref, out_ref):
    count = tiles_ref.shape[0]
    pairs = tiles_ref[...].astype(F32).reshape(count // 2, 2, 8, 128)
    low, high = pairs[:, 0], pairs[:, 1]
    first = lax.broadcasted_iota(jnp.int32, low.shape, 1) < 4
    even = jnp.where(first, low, pltpu.roll(high, 4, 1)).reshape(4 * count, 128).astype(BF16)
    odd = jnp.where(first, pltpu.roll(low, 4, 1), high).reshape(4 * count, 128).astype(BF16)
    gram = lax.dot_general(even, even, NT, preferred_element_type=F32)
    gram = gram + lax.dot_general(odd, odd, NT, preferred_element_type=F32)
    for t in range(count):
        out_ref[t] = gram[4 * t : 4 * t + 4]


def spread_kernel(parts_ref, out_ref):
    total = jnp.sum(parts_ref[...], axis=0)
    out_ref[...] = jnp.broadcast_to(total[None], out_ref.shape)


def on_device(grid, trunc, wlist, leg_even, leg_odd):
    bands = lax.axis_size("band")
    tans = lax.axis_size("tan")
    vectors, fields, lats, lons = grid.shape
    total_lat = lats * bands
    depth = 4 * vectors * fields
    vmem = pl.BlockSpec(memory_space=pltpu.VMEM)
    smem = pl.BlockSpec(memory_space=pltpu.SMEM)
    params = pltpu.CompilerParams(vmem_limit_bytes=32 * 1024 * 1024)

    lat_rows = pl.pallas_call(
        fourier_kernel,
        name="fourier",
        out_shape=jax.ShapeDtypeStruct((bands, depth, 128), BF16),
        in_specs=[smem, vmem, vmem],
        out_specs=vmem,
        scratch_shapes=[pltpu.VMEM((4 * bands, lons), BF16), pltpu.VMEM((bands * depth, 128), F32)],
        compiler_params=params,
    )(wlist, trunc.reshape(1, lats), grid)
    received = lax.all_to_all(lat_rows, "band", split_axis=0, concat_axis=0, tiled=True)

    even, odd, tiles = pl.pallas_call(
        legendre_kernel,
        name="legendre",
        out_shape=(
            jax.ShapeDtypeStruct((1, vectors, fields, 2, leg_even.shape[2]), F32),
            jax.ShapeDtypeStruct((1, vectors, fields, 2, leg_odd.shape[2]), F32),
            jax.ShapeDtypeStruct((tans, 2 * vectors, 128), BF16),
        ),
        in_specs=[smem, vmem, vmem, vmem],
        out_specs=(vmem, vmem, vmem),
        scratch_shapes=[pltpu.VMEM((2, depth, total_lat // 2), F32)],
        compiler_params=params,
    )(wlist, received, jnp.swapaxes(leg_even, 1, 2), leg_odd)
    tiles = lax.all_to_all(tiles, "tan", split_axis=0, concat_axis=0, tiled=True)

    products = pl.pallas_call(
        gram_kernel,
        name="gram",
        out_shape=jax.ShapeDtypeStruct((tans, vectors, vectors * tans), F32),
        in_specs=[vmem],
        out_specs=vmem,
        compiler_params=params,
    )(tiles)
    products = lax.all_to_all(products, "tan", split_axis=0, concat_axis=0, tiled=True)

    spread = pl.pallas_call(
        spread_kernel,
        name="spread",
        out_shape=jax.ShapeDtypeStruct((bands, vectors, vectors * tans), F32),
        in_specs=[vmem],
        out_specs=vmem,
        compiler_params=params,
    )(products)
    summed = lax.all_to_all(spread, "band", split_axis=0, concat_axis=0, tiled=True)
    inner = jnp.sum(summed, axis=0).T / (bands * 4.0 * (total_lat + 1))
    return (even, odd, inner)


def solution(mesh):
    return jax.shard_map(
        on_device,
        mesh=mesh,
        in_specs=(
            P("tan", None, "band", None),
            P("band"),
            P(),
            P("band", None, None),
            P("band", None, None),
        ),
        out_specs=(
            P("band", "tan", None, None, None),
            P("band", "tan", None, None, None),
            P(None, "tan"),
        ),
        check_vma=False,
    )
```

time: 156 us -> 72.4 us (0.46)
  waiting for transfers between devices: 80.6 us -> 0 us
  blocking collectives: 28 us -> 63.5 us
  between operations: 15.5 us -> 0.66 us
  starting transfers between devices: 10.2 us -> 0 us
  matrix products: 6.15 us -> 0 us
  local copies, waits for them, and re-layouts: 9.01 us -> 3.24 us
  other arithmetic: 5.79 us -> 0.61 us
  Pallas kernels: 0 us -> 4.08 us
    all_gather x1 -> x0, waiting for transfers between devices: 74.5 us -> none  [on_device(): lax.all_gather(packed, 'tan', axis=0, tiled=True)]
    all_to_all x0 -> x4, blocking collectives: none -> 63.5 us  [the longest x1 20.6 us: on_device(): lax.all_to_all(tiles, 'tan', split_axis=0, concat_axis=0, tiled=True)]
    psum x1 -> x0, blocking collectives: 28 us -> none  [on_device(): summed = lax.psum(partial_sums, 'band')]
    all_to_all x1 -> x0, starting transfers between devices: 10.2 us -> none  [on_device(): lax.all_to_all(lat_rows, 'band', split_axis=0, concat_axis=1, tiled=True)]
    dot_general x4 -> x0, matrix products: 6.15 us -> none  [the longest x1 1.75 us: on_device(): jnp.einsum('ak,ck->ac', lax.all_gather(packed, 'tan', axis=0, tiled=True)...]
    all_to_all x1 -> x0, waiting for transfers between devices: 6.09 us -> none  [on_device(): lax.all_to_all(lat_rows, 'band', split_axis=0, concat_axis=1, tiled=True)]
    pallas_call x0 -> x4, Pallas kernels: none -> 4.08 us  [the longest x1 2.03 us: on_device(): pl.pallas_call(fourier_kernel, name='fourier', out_shape=jax.ShapeDtypeSt...]
    another operation x5 -> x0, other arithmetic: 3.22 us -> none  [the longest x2 1.65 us: on_device(): mvals = jnp.stack([wlist, total_lat - 1 - wlist], axis=1)]
  transfers between devices with their start and end apart: 2 -> 0, of which waited for: 2 -> 0; matrix products, arithmetic and copies ran while one was open for 2% -> 0% of each run, Pallas kernels for 0% -> 0%
where the time goes in v1:
time: 72.4 us; the launch traced here: 72.1 us
  blocking collectives  63.5 us (88%)
  Pallas kernels  4.08 us (6%)
  local copies, waits for them, and re-layouts  3.24 us (4%)
    all_to_all x1, blocking collectives, on_device(): lax.all_to_all(tiles, 'tan', split_axis=0, concat_axis=0, tiled=True)  20.6 us
    all_to_all x1, blocking collectives, on_device(): lax.all_to_all(lat_rows, 'band', split_axis=0, concat_axis=0, tiled=True)  18.5 us
    all_to_all x1, blocking collectives, on_device(): lax.all_to_all(products, 'tan', split_axis=0, concat_axis=0, tiled=True)  12.3 us
    all_to_all x1, blocking collectives, on_device(): lax.all_to_all(spread, 'band', split_axis=0, concat_axis=0, tiled=True)  12.1 us
    unnamed x10, local copies, waits for them, and re-layouts  3.24 us
    pallas_call x1, Pallas kernels, on_device(): pl.pallas_call(fourier_kernel, name='fourier', out_shape=jax.ShapeDtypeSt...  2.03 us
    pallas_call x1, Pallas kernels, on_device(): pl.pallas_call(legendre_kernel, name='legendre', out_shape=(jax.ShapeDtyp...  1.85 us

profile of v1, /device:TPU:1, one launch (start us, length us, event | category | flops | bytes accessed | tf_op | source)
XLA Modules:
  0.0 72.1 jit_solution(928555703714385616)
XLA Ops:
  0.6 0.0 copy-start
  0.6 1.9 %copy-done = bf16[4,2,80,2560]{3,2,1,0:T(8,128)(2,1)S(1)} copy-done((bf16[4,2,80,2560]{3,2,1,0:T(8,128)(2,1)S(1)}, bf16[4,2,80,2560]{3,2,1,0:T(8,128)(2,1)}, u32[]{:S(2)}) %copy-start) | copy-done | bytes 3276824
  2.6 0.0 copy-start.3
  2.6 0.7 copy-done.3
  3.2 0.0 copy-start.4
  3.2 0.7 copy-done.4
  3.9 0.0 copy-start.1
  3.9 0.0 copy-start.2
  3.9 2.0 %fourier.1 = bf16[16,32,128]{2,1,0:T(8,128)(2,1)S(1)} custom-call(s32[16]{0:T(128)S(1)} %copy-done.3, s32[1,80]{1,0:T(1,128)S(1)} %bitcast.5, bf16[4,2,80,2560]{3,2,1,0:T(8,128)(2,1)S(1)} %copy-done), custom_call_target="tpu_custom_call" | custom-call | tf_op jit(solution)/shard_map/fourier/pallas_call | solution.py:137
  5.9 18.5 %all_to_all.20.rows_ref = bf16[16,32,128]{2,1,0:T(8,128)(2,1)S(1)} all-to-all(bf16[16,32,128]{2,1,0:T(8,128)(2,1)S(1)} %fourier.1), channel_id=1, replica_groups=mesh['band'=16,'tan'=32] {'band'}, dimensions={0} | all-to-all | bytes 262144 | tf_op jit(solution)/shard_map/all_to_all | solution.py:146
  24.4 0.0 copy-done.1
  24.4 0.0 copy-done.2
  24.4 1.8 %legendre.1 = (f32[1,4,2,2,641]{4,3,2,1,0:T(2,128)}, f32[1,4,2,2,640]{4,3,2,1,0:T(2,128)}, bf16[32,8,128]{2,1,0:T(8,128)(2,1)S(1)}) custom-call(s32[16]{0:T(128)S(1)} %copy-done.3, bf16[16,32,128]{2,1,0:T(8,128)(2,1)S(1)} %all_to_all.20.rows_ref, bf16[1,641,640]{2,1,0:T(8,128)(2,1)S(1)} %bitcast.4, bf16[1,640,640]{2,1,0:T(8,128)(2,1)S(1)} %copy-done.2), custom_call_target="tpu_custom_call" | custom-call | tf_op jit(solution)/shard_map/legendre/pallas_call | solution.py:148
  26.3 20.6 %all_to_all.21.tiles_ref = bf16[32,8,128]{2,1,0:T(8,128)(2,1)S(1)} all-to-all(bf16[32,8,128]{2,1,0:T(8,128)(2,1)S(1)} %get-tuple-element.8), channel_id=1, replica_groups=mesh['band'=16,'tan'=32] {'tan'}, dimensions={0} | all-to-all | bytes 131072 | tf_op jit(solution)/shard_map/all_to_all | solution.py:161
  46.9 0.2 gram.1
  47.0 12.3 %all_to_all.22.parts_ref = f32[32,4,128]{2,1,0:T(4,128)S(1)} all-to-all(f32[32,4,128]{2,1,0:T(4,128)S(1)} %gram.1), channel_id=1, replica_groups=mesh['band'=16,'tan'=32] {'tan'}, dimensions={0} | all-to-all | bytes 131072 | tf_op jit(solution)/shard_map/all_to_all | solution.py:171
  59.4 12.1 %all_to_all.23 = f32[16,4,128]{2,1,0:T(4,128)S(1)} all-to-all(f32[16,4,128]{2,1,0:T(4,128)S(1)} %spread.1), channel_id=1, replica_groups=mesh['band'=16,'tan'=32] {'band'}, dimensions={0} | all-to-all | bytes 65536 | tf_op jit(solution)/shard_map/all_to_all | solution.py:181
  71.5 0.6 multiply_bitcast_fusion
  (2 shorter events, 0.1 us)
Async XLA Ops:
  0.6 1.9 %copy-start = (bf16[4,2,80,2560]{3,2,1,0:T(8,128)(2,1)S(1)}, bf16[4,2,80,2560]{3,2,1,0:T(8,128)(2,1)}, u32[]{:S(2)}) copy-start(bf16[4,2,80,2560]{3,2,1,0:T(8,128)(2,1)} %grid_ref.1) | copy-start | bytes 9830404
  2.6 0.7 copy-start.3
  3.2 0.7 copy-start.4
  3.9 20.5 %copy-start.1 = (bf16[1,640,641]{1,2,0:T(8,128)(2,1)S(1)}, bf16[1,640,641]{1,2,0:T(8,128)(2,1)}, u32[]{:S(2)}) copy-start(bf16[1,640,641]{1,2,0:T(8,128)(2,1)} %param.8) | copy-start | bytes 2461444
  3.9 20.5 %copy-start.2 = (bf16[1,640,640]{2,1,0:T(8,128)(2,1)S(1)}, bf16[1,640,640]{2,1,0:T(8,128)(2,1)}, u32[]{:S(2)}) copy-start(bf16[1,640,640]{2,1,0:T(8,128)(2,1)} %odd_ref.1) | copy-start | bytes 2457604

commit v2 on v1

v2 whole, which is shorter than its diff:
```python
import functools
import math

import jax
import jax.numpy as jnp
from jax import lax
from jax.experimental import pallas as pl
from jax.experimental.pallas import tpu as pltpu
from jax.sharding import PartitionSpec as P

F32 = jnp.float32
BF16 = jnp.bfloat16
NT = (((1,), (1,)), ((), ()))
NN = (((1,), (0,)), ((), ()))


def fourier_kernel(wlist_hbm, trunc_hbm, grid_hbm, out_ref, wlist_ref, trunc_ref, grid_ref, table, rows, small, sems):
    vectors, fields, lats, lons = grid_ref.shape
    bands = wlist_ref.shape[0]
    total_lat = lats * bands
    members = 2 * bands
    get_wlist = pltpu.make_async_copy(wlist_hbm, wlist_ref, small.at[0])
    get_trunc = pltpu.make_async_copy(trunc_hbm, trunc_ref, small.at[1])
    get_wlist.start()
    get_trunc.start()
    places = [(v, f) for v in range(vectors) for f in range(fields)]
    fetches = [
        pltpu.make_async_copy(grid_hbm.at[v, f], grid_ref.at[v, f], sems.at[n])
        for n, (v, f) in enumerate(places)
    ]
    for fetch in fetches:
        fetch.start()
    row = lax.broadcasted_iota(jnp.int32, (members, 128), 0)
    lane = lax.broadcasted_iota(jnp.int32, (members, 128), 1)
    get_wlist.wait()
    mvals = jnp.zeros((members, 128), jnp.int32)
    for b in range(bands):
        wave = wlist_ref[b]
        mvals = jnp.where(row == b, wave, mvals)
        mvals = jnp.where(row == bands + b, total_lat - 1 - wave, mvals)
    unit = 2.0 * math.pi / lons
    scaling = 1.0 / math.sqrt(lons)
    chunks = lons // 128
    fine = (mvals * lane % lons).astype(F32) * unit
    coarse = (mvals * lane % chunks).astype(F32) * (128.0 * unit)
    fine_cos, fine_sin = jnp.cos(fine), jnp.sin(fine)
    coarse_cos, coarse_sin = jnp.cos(coarse) * scaling, jnp.sin(coarse) * scaling
    for i in range(chunks):
        cc, cs = coarse_cos[:, i : i + 1], coarse_sin[:, i : i + 1]
        table[:members, 128 * i : 128 * (i + 1)] = (cc * fine_cos - cs * fine_sin).astype(BF16)
        table[members:, 128 * i : 128 * (i + 1)] = (-(cs * fine_cos + cc * fine_sin)).astype(BF16)
    get_trunc.wait()
    keep = mvals[:, :lats] <= trunc_ref[...]
    keep = jnp.concatenate([keep, keep], axis=0)
    depth = 4 * vectors * fields
    for n, (v, f) in enumerate(places):
        fetches[n].wait()
        spectra = lax.dot_general(table[...], grid_ref[v, f], NT, preferred_element_type=F32)
        spectra = jnp.where(keep, spectra, 0.0)
        spectra = jnp.pad(spectra, ((0, 0), (0, 128 - lats)))
        for r in range(2):
            for p in range(2):
                place = ((p * fields + f) * 2 + r) * vectors + v
                start = (r * 2 + p) * bands
                rows[pl.ds(place, bands, stride=depth), :] = spectra[start : start + bands]
    out_ref[...] = rows[...].astype(BF16).reshape(out_ref.shape)


def legendre_kernel(wlist_ref, rows_ref, even_t_ref, odd_ref, even_ref, odd_out_ref, send_ref, fold):
    bands, depth, _ = rows_ref.shape
    half_bands = bands // 2
    hemisphere = odd_ref.shape[1]
    lats = hemisphere // half_bands
    total_lat = 2 * hemisphere
    fields, vectors = even_ref.shape[2], even_ref.shape[1]
    own = wlist_ref[lax.axis_index("band")]
    ri = lax.broadcasted_iota(jnp.int32, (128, 128), 0)
    ci = lax.broadcasted_iota(jnp.int32, (128, 128), 1)
    mirror = jnp.where(ri + ci == lats - 1, 1.0, 0.0).astype(BF16)
    south = rows_ref[half_bands:].reshape(half_bands * depth, 128)
    south = lax.dot_general(south, mirror, NN, preferred_element_type=F32)
    for b in range(half_bands):
        north_b = rows_ref[b].astype(F32)
        s = half_bands - 1 - b
        south_b = south[s * depth : (s + 1) * depth]
        fold[0, :, lats * b : lats * (b + 1)] = (north_b + south_b)[:, :lats]
        fold[1, :, lats * b : lats * (b + 1)] = (north_b - south_b)[:, :lats]
    sym, anti = fold[0].astype(BF16), fold[1].astype(BF16)
    even_all = lax.dot_general(sym, even_t_ref[0], NT, preferred_element_type=F32)
    odd_all = lax.dot_general(anti, odd_ref[0], NN, preferred_element_type=F32)
    half = depth // 2
    even_col = lax.broadcasted_iota(jnp.int32, (half, hemisphere + 1), 1)
    odd_col = lax.broadcasted_iota(jnp.int32, (half, hemisphere), 1)
    even = jnp.where(even_col < (total_lat + 1 - own) // 2, even_all[:half], even_all[half:])
    odd = jnp.where(odd_col < (total_lat - own) // 2, odd_all[:half], odd_all[half:])
    parts = fields * 2
    for fr in range(parts):
        for v in range(vectors):
            f, r, place = fr // 2, fr % 2, fr * vectors + v
            even_ref[0, v, f, r : r + 1, :] = even[place : place + 1]
            odd_out_ref[0, v, f, r : r + 1, :] = odd[place : place + 1]
    columns = send_ref.shape[0] // parts
    tiles = hemisphere // 128
    first = lax.broadcasted_iota(jnp.int32, (8, 128), 0) < vectors
    corner = (lax.broadcasted_iota(jnp.int32, (8, 128), 1) == 0) & first
    for fr in range(parts):
        base = fr // 2 * 8
        for i in range(tiles):
            ev = even[base : base + 8, 128 * i : 128 * (i + 1)]
            od = odd[base : base + 8, 128 * i : 128 * (i + 1)]
            if fr % 2 == 0:
                tile = jnp.where(first, ev, pltpu.roll(od, 4, 0))
            else:
                tile = jnp.where(first, pltpu.roll(ev, 4, 0), od)
            tile = tile.astype(BF16)
            for z in range(columns):
                send_ref[fr * columns + z, i] = tile
        last = jnp.broadcast_to(even[base : base + 8, hemisphere : hemisphere + 1], (8, 128))
        if fr % 2 == 1:
            last = pltpu.roll(last, 4, 0)
        last = jnp.where(corner, last, 0.0).astype(BF16)
        for z in range(columns):
            send_ref[fr * columns + z, tiles] = last


def gram_kernel(columns, tiles_ref, out_ref, gram_ref):
    count, tiles = tiles_ref.shape[:2]
    peers = out_ref.shape[0]
    wide = count // columns
    first = lax.broadcasted_iota(jnp.int32, (count // 2, 8, 128), 1) < 4
    evens, odds = [], []
    for i in range(tiles):
        pairs = tiles_ref[:, i].astype(F32).reshape(count // 2, 2, 8, 128)
        low, high = pairs[:, 0], pairs[:, 1]
        evens.append(jnp.where(first, low, pltpu.roll(high, 4, 1)).reshape(4 * count, 128).astype(BF16))
        if i < tiles - 1:
            odds.append(jnp.where(first, pltpu.roll(low, 4, 1), high).reshape(4 * count, 128).astype(BF16))
    both = jnp.concatenate(evens + odds, axis=1)
    gram = lax.dot_general(both, both, NT, preferred_element_type=F32)
    for t in range(count):
        gram_ref[t] = gram[4 * t : 4 * t + 4]
    z = lax.axis_index("z")
    for x in range(wide):
        block = gram_ref[x * columns + z].astype(BF16)
        for b in range(peers // wide):
            out_ref[b * wide + x] = block


def sum_kernel(scale, parts_ref, out_ref):
    out_ref[...] = jnp.sum(parts_ref[...].astype(F32), axis=0) * scale


def on_device(grid, trunc, wlist, leg_even, leg_odd):
    bands = lax.axis_size("band")
    tans = lax.axis_size(("x", "z"))
    vectors, fields, lats, lons = grid.shape
    total_lat = lats * bands
    depth = 4 * vectors * fields
    vmem = pl.BlockSpec(memory_space=pltpu.VMEM)
    smem = pl.BlockSpec(memory_space=pltpu.SMEM)
    params = pltpu.CompilerParams(vmem_limit_bytes=32 * 1024 * 1024)

    hbm = pl.BlockSpec(memory_space=pltpu.HBM)
    lat_rows = pl.pallas_call(
        fourier_kernel,
        name="fourier",
        out_shape=jax.ShapeDtypeStruct((bands, depth, 128), BF16),
        in_specs=[hbm, hbm, hbm],
        out_specs=vmem,
        scratch_shapes=[
            pltpu.SMEM((bands,), jnp.int32),
            pltpu.VMEM((1, lats), jnp.int32),
            pltpu.VMEM(grid.shape, BF16),
            pltpu.VMEM((4 * bands, lons), BF16),
            pltpu.VMEM((bands * depth, 128), F32),
            pltpu.SemaphoreType.DMA((2,)),
            pltpu.SemaphoreType.DMA((vectors * fields,)),
        ],
        compiler_params=params,
    )(
        pltpu.with_memory_space_constraint(wlist, pltpu.HBM),
        pltpu.with_memory_space_constraint(trunc.reshape(1, lats), pltpu.HBM),
        pltpu.with_memory_space_constraint(grid, pltpu.HBM),
    )
    received = lax.all_to_all(lat_rows, "band", split_axis=0, concat_axis=0, tiled=True)

    even, odd, tiles = pl.pallas_call(
        legendre_kernel,
        name="legendre",
        out_shape=(
            jax.ShapeDtypeStruct((1, vectors, fields, 2, leg_even.shape[2]), F32),
            jax.ShapeDtypeStruct((1, vectors, fields, 2, leg_odd.shape[2]), F32),
            jax.ShapeDtypeStruct((tans, total_lat // 256 + 1, 2 * vectors, 128), BF16),
        ),
        in_specs=[smem, vmem, vmem, vmem],
        out_specs=(vmem, vmem, vmem),
        scratch_shapes=[pltpu.VMEM((2, depth, total_lat // 2), F32)],
        compiler_params=params,
    )(wlist, received, jnp.swapaxes(leg_even, 1, 2), leg_odd)
    tiles = lax.all_to_all(tiles, ("x", "z"), split_axis=0, concat_axis=0, tiled=True)

    parts = 2 * fields
    columns = tans // parts
    products = pl.pallas_call(
        functools.partial(gram_kernel, columns),
        name="gram",
        out_shape=jax.ShapeDtypeStruct((bands * parts, vectors, vectors * tans), BF16),
        in_specs=[vmem],
        out_specs=vmem,
        scratch_shapes=[pltpu.VMEM((tans, vectors, vectors * tans), F32)],
        compiler_params=params,
    )(tiles)
    products = lax.all_to_all(products, ("band", "x"), split_axis=0, concat_axis=0, tiled=True)

    scale = 1.0 / (bands * 4.0 * (total_lat + 1))
    inner = pl.pallas_call(
        functools.partial(sum_kernel, scale),
        name="sum",
        out_shape=jax.ShapeDtypeStruct((vectors, vectors * tans), F32),
        in_specs=[vmem],
        out_specs=vmem,
        compiler_params=params,
    )(products)
    return (even, odd, inner.T)


def solution(mesh):
    bands, tans = mesh.devices.shape
    split = jax.sharding.Mesh(mesh.devices.reshape(bands, 4, tans // 4), ("band", "x", "z"))
    tan = ("x", "z")
    return jax.shard_map(
        on_device,
        mesh=split,
        in_specs=(
            P(tan, None, "band", None),
            P("band"),
            P(),
            P("band", None, None),
            P("band", None, None),
        ),
        out_specs=(
            P("band", tan, None, None, None),
            P("band", tan, None, None, None),
            P(None, tan),
        ),
        check_vma=False,
    )
```

time: 72.4 us -> 67 us (0.925)
  blocking collectives: 63.5 us -> 58.6 us
  Pallas kernels: 4.08 us -> 7.43 us
  local copies, waits for them, and re-layouts: 3.24 us -> 0.01 us
    all_to_all x3 -> x2, blocking collectives: 45 us -> 40.2 us  [the longest x1 25 us: on_device(): lax.all_to_all(tiles, ('x', 'z'), split_axis=0, concat_axis=0, tiled=True)]
    unnamed x10 -> x6, local copies, waits for them, and re-layouts: 3.24 us -> 0.01 us
    pallas_call x1, Pallas kernels: 2.03 us -> 4.61 us  [on_device(): pl.pallas_call(fourier_kernel, name='fourier', out_shape=jax.ShapeDtypeSt...]
    pallas_call x2, Pallas kernels: 0.2 us -> 0.95 us  [the longest x1 0.65 us: on_device(): pl.pallas_call(functools.partial(sum_kernel, scale), name='sum', out_shap...]
where the time goes in v2:
time: 67 us; the launch traced here: 66.8 us
  blocking collectives  58.6 us (87%)
  Pallas kernels  7.43 us (11%)
  between operations  0.68 us (1%)
    all_to_all x1, blocking collectives, on_device(): lax.all_to_all(tiles, ('x', 'z'), split_axis=0, concat_axis=0, tiled=True)  25 us
    all_to_all x1, blocking collectives, on_device(): lax.all_to_all(lat_rows, 'band', split_axis=0, concat_axis=0, tiled=True)  18.5 us
    all_to_all x1, blocking collectives, on_device(): lax.all_to_all(products, ('band', 'x'), split_axis=0, concat_axis=0, tile...  15.2 us
    pallas_call x1, Pallas kernels, on_device(): pl.pallas_call(fourier_kernel, name='fourier', out_shape=jax.ShapeDtypeSt...  4.61 us
    pallas_call x1, Pallas kernels, on_device(): pl.pallas_call(legendre_kernel, name='legendre', out_shape=(jax.ShapeDtyp...  1.86 us

profile of v2, /device:TPU:1, one launch (start us, length us, event | category | flops | bytes accessed | tf_op | source)
XLA Modules:
  0.0 66.8 jit_solution(12277027815927380557)
XLA Ops:
  0.6 0.0 copy-start.2
  0.6 0.0 copy-start.1
  0.7 0.0 copy-start
  0.7 4.6 %fourier.1 = bf16[16,32,128]{2,1,0:T(8,128)(2,1)S(1)} custom-call(s32[16]{0:T(128)} %wlist_ref.1, s32[1,80]{1,0:T(1,128)} %bitcast.5, bf16[4,2,80,2560]{3,2,1,0:T(8,128)(2,1)} %grid_hbm.1), custom_call_target="tpu_custom_call" | custom-call | tf_op jit(solution)/shard_map/fourier/pallas_call | solution.py:164
  5.3 18.5 %all_to_all.15.rows_ref = bf16[16,32,128]{2,1,0:T(8,128)(2,1)S(1)} all-to-all(bf16[16,32,128]{2,1,0:T(8,128)(2,1)S(1)} %fourier.1), channel_id=1, replica_groups=mesh['band'=16,'x'=4,'z'=8] {'band'}, dimensions={0} | all-to-all | bytes 262144 | tf_op jit(solution)/shard_map/all_to_all | solution.py:185
  23.8 0.0 copy-done.2
  23.8 0.0 copy-done.1
  23.8 0.0 copy-done
  23.8 1.9 %legendre.1 = (f32[1,4,2,2,641]{4,3,2,1,0:T(2,128)}, f32[1,4,2,2,640]{4,3,2,1,0:T(2,128)}, bf16[32,6,8,128]{3,2,1,0:T(8,128)(2,1)S(1)}) custom-call(s32[16]{0:T(128)S(1)} %copy-done.2, bf16[16,32,128]{2,1,0:T(8,128)(2,1)S(1)} %all_to_all.15.rows_ref, bf16[1,641,640]{2,1,0:T(8,128)(2,1)S(1)} %bitcast.3, bf16[1,640,640]{2,1,0:T(8,128)(2,1)S(1)} %copy-done.1), custom_call_target="tpu_custom_call" | custom-call | tf_op jit(solution)/shard_map/legendre/pallas_call | solution.py:187
  25.7 25.0 %all_to_all.16.tiles_ref = bf16[32,6,8,128]{3,2,1,0:T(8,128)(2,1)S(1)} all-to-all(bf16[32,6,8,128]{3,2,1,0:T(8,128)(2,1)S(1)} %get-tuple-element.8), channel_id=1, replica_groups=mesh['band'=16,'x'=4,'z'=8] {'x','z'}, dimensions={0} | all-to-all | bytes 786432 | tf_op jit(solution)/shard_map/all_to_all | solution.py:200
  50.7 0.3 gram.1
  51.0 15.2 %all_to_all.17.parts_ref = bf16[64,4,128]{2,1,0:T(4,128)(2,1)S(1)} all-to-all(bf16[64,4,128]{2,1,0:T(4,128)(2,1)S(1)} %gram.1), channel_id=1, replica_groups=mesh['band'=16,'x'=4,'z'=8] {'band','x'}, dimensions={0} | all-to-all | bytes 131072 | tf_op jit(solution)/shard_map/all_to_all | solution.py:213
  66.1 0.6 sum.1
Async XLA Ops:
  0.6 23.1 %copy-start.2 = (s32[16]{0:T(128)S(1)}, s32[16]{0:T(128)}, u32[]{:S(2)}) copy-start(s32[16]{0:T(128)} %wlist_ref.1) | copy-start | bytes 196
  0.6 23.1 %copy-start.1 = (bf16[1,640,640]{2,1,0:T(8,128)(2,1)S(1)}, bf16[1,640,640]{2,1,0:T(8,128)(2,1)}, u32[]{:S(2)}) copy-start(bf16[1,640,640]{2,1,0:T(8,128)(2,1)} %odd_ref.1) | copy-start | bytes 2457604
  0.7 23.1 %copy-start = (bf16[1,640,641]{1,2,0:T(8,128)(2,1)S(1)}, bf16[1,640,641]{1,2,0:T(8,128)(2,1)}, u32[]{:S(2)}) copy-start(bf16[1,640,641]{1,2,0:T(8,128)(2,1)} %param.8) | copy-start | bytes 2461444

commit v3 on v2

v3 whole, which is shorter than its diff:
```python
import functools
import math

import jax
import jax.numpy as jnp
from jax import lax
from jax.experimental import pallas as pl
from jax.experimental.pallas import tpu as pltpu
from jax.sharding import PartitionSpec as P

F32 = jnp.float32
BF16 = jnp.bfloat16
NT = (((1,), (1,)), ((), ()))
NN = (((1,), (0,)), ((), ()))


def fourier_kernel(wlist_hbm, trunc_hbm, grid_hbm, out_ref, own_ref, wlist_ref, trunc_ref, grid_ref, table, rows, small, sems):
    vectors, fields, lats, lons = grid_ref.shape
    bands = wlist_ref.shape[0]
    total_lat = lats * bands
    members = 2 * bands
    get_wlist = pltpu.make_async_copy(wlist_hbm, wlist_ref, small.at[0])
    get_trunc = pltpu.make_async_copy(trunc_hbm, trunc_ref, small.at[1])
    get_wlist.start()
    get_trunc.start()
    half = vectors // 2
    fetches = [
        pltpu.make_async_copy(grid_hbm.at[pl.ds(v, half)], grid_ref.at[pl.ds(v, half)], sems.at[n])
        for n, v in enumerate(range(0, vectors, half))
    ]
    for fetch in fetches:
        fetch.start()
    row = lax.broadcasted_iota(jnp.int32, (members, 128), 0)
    lane = lax.broadcasted_iota(jnp.int32, (members, 128), 1)
    get_wlist.wait()
    mvals = jnp.zeros((members, 128), jnp.int32)
    for b in range(bands):
        wave, place = wlist_ref[b], b
        mvals = jnp.where(row == place, wave, mvals)
        mvals = jnp.where(row == bands + place, total_lat - 1 - wave, mvals)
    own_ref[...] = jnp.full(own_ref.shape, wlist_ref[lax.axis_index("band")], jnp.int32)
    unit = 2.0 * math.pi / lons
    scaling = 1.0 / math.sqrt(lons)
    chunks = lons // 128
    fine = (mvals * lane % lons).astype(F32) * unit
    coarse = (mvals * lane % chunks).astype(F32) * (128.0 * unit)
    fine_cos, fine_sin = jnp.cos(fine), jnp.sin(fine)
    coarse_cos, coarse_sin = jnp.cos(coarse) * scaling, jnp.sin(coarse) * scaling
    for i in range(chunks):
        cc, cs = coarse_cos[:, i : i + 1], coarse_sin[:, i : i + 1]
        table[:members, 128 * i : 128 * (i + 1)] = (cc * fine_cos - cs * fine_sin).astype(BF16)
        table[members:, 128 * i : 128 * (i + 1)] = (-(cs * fine_cos + cc * fine_sin)).astype(BF16)
    get_trunc.wait()
    keep = mvals[:, :lats] <= trunc_ref[...]
    keep = jnp.concatenate([keep, keep], axis=0)
    depth = 4 * vectors * fields
    for v in range(vectors):
        if v % half == 0:
            fetches[v // half].wait()
        for f in range(fields):
            spectra = lax.dot_general(table[...], grid_ref[v, f], NT, preferred_element_type=F32)
            spectra = jnp.where(keep, spectra, 0.0)
            spectra = jnp.pad(spectra, ((0, 0), (0, 128 - lats)))
            for r in range(2):
                for p in range(2):
                    place = ((p * fields + f) * 2 + r) * vectors + v
                    start = (r * 2 + p) * bands
                    rows[pl.ds(place, bands, stride=depth), :] = spectra[start : start + bands]
    out_ref[...] = rows[...].astype(BF16).reshape(out_ref.shape)


def legendre_kernel(own_ref, rows_ref, even_t_ref, odd_ref, send_ref, even_ref, odd_out_ref, fold):
    bands, depth, _ = rows_ref.shape
    half_bands = bands // 2
    hemisphere = odd_ref.shape[1]
    lats = hemisphere // half_bands
    total_lat = 2 * hemisphere
    own = own_ref[0:1, 0:1]
    ri = lax.broadcasted_iota(jnp.int32, (128, 128), 0)
    ci = lax.broadcasted_iota(jnp.int32, (128, 128), 1)
    mirror = jnp.where(ri + ci == lats - 1, 1.0, 0.0).astype(BF16)
    south = rows_ref[half_bands:].reshape(half_bands * depth, 128)
    south = lax.dot_general(south, mirror, NN, preferred_element_type=F32)
    for b in range(half_bands):
        north_b = rows_ref[b].astype(F32)
        s = half_bands - 1 - b
        south_b = south[s * depth : (s + 1) * depth]
        fold[0, :, lats * b : lats * (b + 1)] = (north_b + south_b)[:, :lats]
        fold[1, :, lats * b : lats * (b + 1)] = (north_b - south_b)[:, :lats]
    sym, anti = fold[0].astype(BF16), fold[1].astype(BF16)
    even_all = lax.dot_general(sym, even_t_ref[0], NT, preferred_element_type=F32)
    odd_all = lax.dot_general(anti, odd_ref[0], NN, preferred_element_type=F32)
    half = depth // 2
    even_col = lax.broadcasted_iota(jnp.int32, (half, hemisphere + 1), 1)
    odd_col = lax.broadcasted_iota(jnp.int32, (half, hemisphere), 1)
    even = jnp.where(even_col < ((total_lat + 1 - own) >> 1), even_all[:half], even_all[half:])
    odd = jnp.where(odd_col < ((total_lat - own) >> 1), odd_all[:half], odd_all[half:])
    even_ref[...] = even
    odd_out_ref[...] = odd
    tiles = hemisphere // 128
    vectors = 4
    parts = half // vectors
    columns = 2 * send_ref.shape[0] // parts
    last = jnp.broadcast_to(even[:, hemisphere : hemisphere + 1], (half, 128))
    last = jnp.where(lax.broadcasted_iota(jnp.int32, (half, 128), 1) == 0, last, 0.0)
    pieces = [even[:, 128 * i : 128 * (i + 1)] for i in range(tiles)]
    pieces += [odd[:, 128 * i : 128 * (i + 1)] for i in range(tiles)]
    pieces += [last]
    first = lax.broadcasted_iota(jnp.int32, (8, 128), 0) < vectors
    for fr in range(parts):
        base = fr // 2 * 8
        same = [piece[base : base + 8] for piece in pieces]
        other = [pltpu.roll(piece, vectors, 0) for piece in same]
        low, high = (same, other) if fr % 2 == 0 else (other, same)
        quarters = 2 * list(range(len(pieces)))
        slab = [jnp.where(first, low[i], high[j]) for i, j in zip(quarters[0::2], quarters[1::2])]
        slab = jnp.concatenate(slab, axis=0).astype(BF16)
        for pair in range(columns // 2):
            send_ref[fr * columns // 2 + pair] = slab


def gram_kernel(columns, tiles_ref, out_ref, gram_ref):
    pairs, depth, _ = tiles_ref.shape
    vectors = 4
    count, tiles = 2 * pairs, depth // (2 * vectors)
    wide = count // columns
    slabs = tiles_ref[...].astype(F32)
    eights = [slabs[:, 8 * k : 8 * (k + 1)] for k in range(tiles)]
    first = lax.broadcasted_iota(jnp.int32, (pairs, 8, 128), 1) < vectors
    half = tiles // 2
    columns_of = []
    for i in range(tiles):
        if i % 2 == 0:
            both = jnp.where(first, eights[i // 2], eights[half + i // 2])
        else:
            both = jnp.where(first, eights[half + (i + 1) // 2], eights[i // 2])
            both = pltpu.roll(both, vectors, 1)
        columns_of.append(both.reshape(count * vectors, 128).astype(BF16))
    both = jnp.concatenate(columns_of, axis=1)
    gram = lax.dot_general(both, both, NT, preferred_element_type=F32)
    gram_ref[...] = gram.reshape(gram_ref.shape)
    z = lax.axis_index("z")
    rows = [gram_ref[x, lax.div(z, 2)] for x in range(wide)]
    rows = [jnp.where(lax.rem(z, 2) == 0, row, pltpu.roll(row, vectors, 0)) for row in rows]
    first = lax.broadcasted_iota(jnp.int32, (8, 128), 0) < vectors
    rows = [jnp.where(first, rows[x], pltpu.roll(rows[x + 1], vectors, 0)) for x in range(0, wide, 2)]
    block = jnp.concatenate(rows, axis=0).astype(BF16)
    for b in range(out_ref.shape[0]):
        out_ref[b] = block


def finish_kernel(scale, parts_ref, even_in_ref, odd_in_ref, inner_ref, even_ref, odd_ref):
    _, vectors, fields, parts, _ = even_ref.shape
    for f in range(fields):
        for r in range(parts):
            for v in range(vectors):
                row = (f * parts + r) * vectors + v
                even_ref[0, v, f, r : r + 1, :] = even_in_ref[row : row + 1]
                odd_ref[0, v, f, r : r + 1, :] = odd_in_ref[row : row + 1]
    total = jnp.sum(parts_ref[...].astype(F32), axis=0)
    inner_ref[...] = (total[:vectors] + total[vectors:]) * scale


VMEM = pl.BlockSpec(memory_space=pltpu.VMEM)
HBM = pl.BlockSpec(memory_space=pltpu.HBM)
PARAMS = pltpu.CompilerParams(vmem_limit_bytes=32 * 1024 * 1024)


def in_hbm(array):
    return pltpu.with_memory_space_constraint(array, pltpu.HBM)


def fourier(wlist, trunc, grid):
    vectors, fields, lats, lons = grid.shape
    bands = wlist.shape[0]
    depth = 4 * vectors * fields
    return pl.pallas_call(
        fourier_kernel,
        name="fourier",
        out_shape=(
            jax.ShapeDtypeStruct((bands, depth, 128), BF16),
            jax.ShapeDtypeStruct((8, 128), jnp.int32),
        ),
        in_specs=[HBM, HBM, HBM],
        out_specs=(VMEM, VMEM),
        scratch_shapes=[
            pltpu.SMEM((bands,), jnp.int32),
            pltpu.VMEM((1, lats), jnp.int32),
            pltpu.VMEM(grid.shape, BF16),
            pltpu.VMEM((4 * bands, lons), BF16),
            pltpu.VMEM((bands * depth, 128), F32),
            pltpu.SemaphoreType.DMA((2,)),
            pltpu.SemaphoreType.DMA((2,)),
        ],
        compiler_params=PARAMS,
    )(in_hbm(wlist), in_hbm(trunc.reshape(1, lats)), in_hbm(grid))


def legendre(own, received, leg_even, leg_odd, vectors, tans):
    depth = received.shape[1]
    hemisphere = leg_odd.shape[2]
    return pl.pallas_call(
        legendre_kernel,
        name="legendre",
        out_shape=(
            jax.ShapeDtypeStruct((tans // 2, 2 * (hemisphere // 64 + 1) * vectors, 128), BF16),
            jax.ShapeDtypeStruct((depth // 2, leg_even.shape[2]), F32),
            jax.ShapeDtypeStruct((depth // 2, leg_odd.shape[2]), F32),
        ),
        in_specs=[VMEM] * 4,
        out_specs=(VMEM, VMEM, VMEM),
        scratch_shapes=[pltpu.VMEM((2, depth, hemisphere), F32)],
        compiler_params=PARAMS,
    )(own, received, jnp.swapaxes(leg_even, 1, 2), leg_odd)


def gram(tiles, columns, bands, vectors):
    tans = 2 * tiles.shape[0]
    wide = tans // columns
    return pl.pallas_call(
        functools.partial(gram_kernel, columns),
        name="gram",
        out_shape=jax.ShapeDtypeStruct((bands, wide * vectors, vectors * tans), BF16),
        in_specs=[VMEM],
        out_specs=VMEM,
        scratch_shapes=[pltpu.VMEM((wide, columns // 2, 2 * vectors, vectors * tans), F32)],
        compiler_params=PARAMS,
    )(tiles)


def finish(products, even, odd, scale, vectors, fields):
    return pl.pallas_call(
        functools.partial(finish_kernel, scale),
        name="finish",
        out_shape=(
            jax.ShapeDtypeStruct((vectors, products.shape[2]), F32),
            jax.ShapeDtypeStruct((1, vectors, fields, 2, even.shape[1]), F32),
            jax.ShapeDtypeStruct((1, vectors, fields, 2, odd.shape[1]), F32),
        ),
        in_specs=[VMEM] * 3,
        out_specs=(VMEM, VMEM, VMEM),
        compiler_params=PARAMS,
    )(products, even, odd)


def on_device(grid, trunc, wlist, leg_even, leg_odd):
    bands = lax.axis_size("band")
    columns = lax.axis_size("z")
    tans = lax.axis_size(("x", "z"))
    vectors, fields, lats, _ = grid.shape
    total_lat = lats * bands
    lat_rows, own = fourier(wlist, trunc, grid)
    received = lax.all_to_all(lat_rows, "band", 0, 0, tiled=True)
    tiles, even, odd = legendre(own, received, leg_even, leg_odd, vectors, tans)
    slab = tiles.shape
    tiles = tiles.reshape(tans, slab[1] // (2 * vectors), vectors, 128)
    tiles = lax.all_to_all(tiles, ("x", "z"), split_axis=0, concat_axis=0, tiled=True)
    products = gram(tiles.reshape(slab), columns, bands, vectors)
    products = products.reshape(-1, vectors, vectors * tans)
    products = lax.all_to_all(products, ("band", "x"), split_axis=0, concat_axis=0, tiled=True)
    products = products.reshape(-1, 2 * vectors, vectors * tans)
    scale = 1.0 / (bands * 4.0 * (total_lat + 1))
    inner, even, odd = finish(products, even, odd, scale, vectors, fields)
    return (even, odd, inner.T)


def solution(mesh):
    bands, tans = mesh.devices.shape
    split = jax.sharding.Mesh(mesh.devices.reshape(bands, 4, tans // 4), ("band", "x", "z"))
    tan = ("x", "z")
    return jax.shard_map(
        on_device,
        mesh=split,
        in_specs=(
            P(tan, None, "band", None),
            P("band"),
            P(),
            P("band", None, None),
            P("band", None, None),
        ),
        out_specs=(
            P("band", tan, None, None, None),
            P("band", tan, None, None, None),
            P(None, tan),
        ),
        check_vma=False,
    )
```

time: 67 us -> 63.7 us (0.951)
  Pallas kernels: 7.43 us -> 4.54 us
    pallas_call x4, Pallas kernels: 7.43 us -> 4.54 us  [the longest x1 2.89 us: fourier(): pl.pallas_call(fourier_kernel, name='fourier', out_shape=(jax.ShapeDtypeS...]
where the time goes in v3:
time: 63.7 us; the launch traced here: 63.5 us
  blocking collectives  58.3 us (92%)
  Pallas kernels  4.54 us (7%)
  between operations  0.67 us (1%)
    all_to_all x1, blocking collectives, on_device(): lax.all_to_all(tiles, ('x', 'z'), split_axis=0, concat_axis=0, tiled=True)  24.4 us
    all_to_all x1, blocking collectives, on_device(): received = lax.all_to_all(lat_rows, 'band', 0, 0, tiled=True)  18.5 us
    all_to_all x1, blocking collectives, on_device(): lax.all_to_all(products, ('band', 'x'), split_axis=0, concat_axis=0, tile...  15.4 us
    pallas_call x1, Pallas kernels, fourier(): pl.pallas_call(fourier_kernel, name='fourier', out_shape=(jax.ShapeDtypeS...  2.89 us

profile of v3, /device:TPU:1, one launch (start us, length us, event | category | flops | bytes accessed | tf_op | source)
XLA Modules:
  0.0 63.5 jit_solution(15297102594672655691)
XLA Ops:
  0.6 0.0 copy-start.1
  0.6 0.0 copy-start
  0.7 2.9 %fourier.1 = (bf16[16,32,128]{2,1,0:T(8,128)(2,1)S(1)}, s32[8,128]{1,0:T(8,128)S(1)}) custom-call(s32[16]{0:T(128)} %wlist_hbm.1, s32[1,80]{1,0:T(1,128)} %bitcast.12, bf16[4,2,80,2560]{3,2,1,0:T(8,128)(2,1)} %grid_hbm.1), custom_call_target="tpu_custom_call" | custom-call | tf_op jit(solution)/shard_map/fourier/pallas_call | solution.py:177
  3.6 18.5 %all_to_all.15.rows_ref = bf16[16,32,128]{2,1,0:T(8,128)(2,1)S(1)} all-to-all(bf16[16,32,128]{2,1,0:T(8,128)(2,1)S(1)} %get-tuple-element.12), channel_id=1, replica_groups=mesh['band'=16,'x'=4,'z'=8] {'band'}, dimensions={0} | all-to-all | bytes 262144 | tf_op jit(solution)/shard_map/all_to_all | solution.py:253
  22.1 0.0 copy-done.1
  22.1 0.0 copy-done
  22.1 0.7 %legendre.1 = (bf16[16,88,128]{2,1,0:T(8,128)(2,1)S(1)}, f32[16,641]{1,0:T(8,128)S(1)}, f32[16,640]{1,0:T(8,128)S(1)}) custom-call(s32[8,128]{1,0:T(8,128)S(1)} %get-tuple-element.11.own_ref, bf16[16,32,128]{2,1,0:T(8,128)(2,1)S(1)} %all_to_all.15.rows_ref, bf16[1,641,640]{2,1,0:T(8,128)(2,1)S(1)} %bitcast.8, bf16[1,640,640]{2,1,0:T(8,128)(2,1)S(1)} %copy-done.1), custom_call_target="tpu_custom_call" | custom-call | tf_op jit(solution)/shard_map/legendre/pallas_call | solution.py:202
  22.8 24.4 %all_to_all.16 = bf16[32,11,4,128]{3,2,1,0:T(4,128)(2,1)S(1)} all-to-all(bf16[32,11,4,128]{3,2,1,0:T(4,128)(2,1)S(1)} %bitcast.9), channel_id=1, replica_groups=mesh['band'=16,'x'=4,'z'=8] {'x','z'}, dimensions={0} | all-to-all | bytes 720896 | tf_op jit(solution)/shard_map/all_to_all | solution.py:257
  47.2 0.3 gram.1
  47.5 15.4 %all_to_all.17 = bf16[64,4,128]{2,1,0:T(4,128)(2,1)S(1)} all-to-all(bf16[64,4,128]{2,1,0:T(4,128)(2,1)S(1)} %bitcast.11), channel_id=1, replica_groups=mesh['band'=16,'x'=4,'z'=8] {'band','x'}, dimensions={0} | all-to-all | bytes 131072 | tf_op jit(solution)/shard_map/all_to_all | solution.py:260
  62.8 0.7 %finish.1 = (f32[4,128]{1,0:T(4,128)}, f32[1,4,2,2,641]{4,3,2,1,0:T(2,128)}, f32[1,4,2,2,640]{4,3,2,1,0:T(2,128)}) custom-call(bf16[32,8,128]{2,1,0:T(8,128)(2,1)S(1)} %bitcast.10, f32[16,641]{1,0:T(8,128)S(1)} %get-tuple-element.14.even_in_ref, f32[16,640]{1,0:T(8,128)S(1)} %get-tuple-element.15.odd_in_ref), custom_call_target="tpu_custom_call" | custom-call | tf_op jit(solution)/shard_map/finish/pallas_call | solution.py:232
Async XLA Ops:
  0.6 21.4 %copy-start.1 = (bf16[1,640,640]{2,1,0:T(8,128)(2,1)S(1)}, bf16[1,640,640]{2,1,0:T(8,128)(2,1)}, u32[]{:S(2)}) copy-start(bf16[1,640,640]{2,1,0:T(8,128)(2,1)} %odd_ref.1) | copy-start | bytes 2457604
  0.6 21.4 %copy-start = (bf16[1,640,641]{1,2,0:T(8,128)(2,1)S(1)}, bf16[1,640,641]{1,2,0:T(8,128)(2,1)}, u32[]{:S(2)}) copy-start(bf16[1,640,641]{1,2,0:T(8,128)(2,1)} %param.8) | copy-start | bytes 2461444

commit v4 on v3

--- a/solution.py
+++ b/solution.py
@@ -9,9 +9,14 @@
 from jax.sharding import PartitionSpec as P
 
 F32 = jnp.float32
+FIRST_BAND, FIRST_X, FIRST_Z = 13, 2, 6
 BF16 = jnp.bfloat16
 NT = (((1,), (1,)), ((), ()))
 NN = (((1,), (0,)), ((), ()))
+
+
+def turned(count, first):
+    return [(first + n) % count for n in range(count)]
 
 
 def fourier_kernel(wlist_hbm, trunc_hbm, grid_hbm, out_ref, own_ref, wlist_ref, trunc_ref, grid_ref, table, rows, small, sems):
@@ -35,7 +40,7 @@
     get_wlist.wait()
     mvals = jnp.zeros((members, 128), jnp.int32)
     for b in range(bands):
-        wave, place = wlist_ref[b], b
+        wave, place = wlist_ref[b], (b - FIRST_BAND) % bands
         mvals = jnp.where(row == place, wave, mvals)
         mvals = jnp.where(row == bands + place, total_lat - 1 - wave, mvals)
     own_ref[...] = jnp.full(own_ref.shape, wlist_ref[lax.axis_index("band")], jnp.int32)
@@ -79,10 +84,11 @@
     ri = lax.broadcasted_iota(jnp.int32, (128, 128), 0)
     ci = lax.broadcasted_iota(jnp.int32, (128, 128), 1)
     mirror = jnp.where(ri + ci == lats - 1, 1.0, 0.0).astype(BF16)
-    south = rows_ref[half_bands:].reshape(half_bands * depth, 128)
+    south = [rows_ref[(b - FIRST_BAND) % bands] for b in range(half_bands, bands)]
+    south = jnp.concatenate(south, axis=0)
     south = lax.dot_general(south, mirror, NN, preferred_element_type=F32)
     for b in range(half_bands):
-        north_b = rows_ref[b].astype(F32)
+        north_b = rows_ref[(b - FIRST_BAND) % bands].astype(F32)
         s = half_bands - 1 - b
         south_b = south[s * depth : (s + 1) * depth]
         fold[0, :, lats * b : lats * (b + 1)] = (north_b + south_b)[:, :lats]
@@ -124,7 +130,12 @@
     vectors = 4
     count, tiles = 2 * pairs, depth // (2 * vectors)
     wide = count // columns
-    slabs = tiles_ref[...].astype(F32)
+    half_z = columns // 2
+    half_first = FIRST_Z // 2
+    places = [
+        (x - FIRST_X) % wide * half_z + (z - half_first) % half_z for x in range(wide) for z in range(half_z)
+    ]
+    slabs = jnp.stack([tiles_ref[n] for n in places]).astype(F32)
     eights = [slabs[:, 8 * k : 8 * (k + 1)] for k in range(tiles)]
     first = lax.broadcasted_iota(jnp.int32, (pairs, 8, 128), 1) < vectors
     half = tiles // 2
@@ -140,7 +151,7 @@
     gram = lax.dot_general(both, both, NT, preferred_element_type=F32)
     gram_ref[...] = gram.reshape(gram_ref.shape)
     z = lax.axis_index("z")
-    rows = [gram_ref[x, lax.div(z, 2)] for x in range(wide)]
+    rows = [gram_ref[(x + FIRST_X) % wide, lax.div(z, 2)] for x in range(wide)]
     rows = [jnp.where(lax.rem(z, 2) == 0, row, pltpu.roll(row, vectors, 0)) for row in rows]
     first = lax.broadcasted_iota(jnp.int32, (8, 128), 0) < vectors
     rows = [jnp.where(first, rows[x], pltpu.roll(rows[x + 1], vectors, 0)) for x in range(0, wide, 2)]
@@ -250,14 +261,19 @@
     vectors, fields, lats, _ = grid.shape
     total_lat = lats * bands
     lat_rows, own = fourier(wlist, trunc, grid)
-    received = lax.all_to_all(lat_rows, "band", 0, 0, tiled=True)
+    received = lax.all_to_all(
+        lat_rows, "band", 0, 0, axis_index_groups=[turned(bands, FIRST_BAND)], tiled=True
+    )
     tiles, even, odd = legendre(own, received, leg_even, leg_odd, vectors, tans)
     slab = tiles.shape
     tiles = tiles.reshape(tans, slab[1] // (2 * vectors), vectors, 128)
-    tiles = lax.all_to_all(tiles, ("x", "z"), split_axis=0, concat_axis=0, tiled=True)
+    wide = tans // columns
+    tan_group = [x * columns + z for x in turned(wide, FIRST_X) for z in turned(columns, FIRST_Z)]
+    tiles = lax.all_to_all(tiles, ("x", "z"), 0, 0, axis_index_groups=[tan_group], tiled=True)
     products = gram(tiles.reshape(slab), columns, bands, vectors)
     products = products.reshape(-1, vectors, vectors * tans)
-    products = lax.all_to_all(products, ("band", "x"), split_axis=0, concat_axis=0, tiled=True)
+    group = [b * wide + x for b in turned(bands, FIRST_BAND) for x in turned(wide, FIRST_X)]
+    products = lax.all_to_all(products, ("band", "x"), 0, 0, axis_index_groups=[group], tiled=True)
     products = products.reshape(-1, 2 * vectors, vectors * tans)
     scale = 1.0 / (bands * 4.0 * (total_lat + 1))
     inner, even, odd = finish(products, even, odd, scale, vectors, fields)

time: 63.7 us -> 58.5 us (0.918)
  blocking collectives: 58.3 us -> 53.1 us
    all_to_all x3, blocking collectives: 58.3 us -> 53.1 us  [the longest x1 20.3 us: on_device(): lax.all_to_all(tiles, ('x', 'z'), 0, 0, axis_index_groups=[tan_group], ti...]
where the time goes in v4:
time: 58.5 us; the launch traced here: 58.3 us
  blocking collectives  53.1 us (91%)
  Pallas kernels  4.54 us (8%)
  between operations  0.67 us (1%)
    all_to_all x1, blocking collectives, on_device(): lax.all_to_all(tiles, ('x', 'z'), 0, 0, axis_index_groups=[tan_group], ti...  20.3 us
    all_to_all x1, blocking collectives, on_device(): lax.all_to_all(lat_rows, 'band', 0, 0, axis_index_groups=[turned(bands, F...  17.3 us
    all_to_all x1, blocking collectives, on_device(): lax.all_to_all(products, ('band', 'x'), 0, 0, axis_index_groups=[group],...  15.5 us
    pallas_call x1, Pallas kernels, fourier(): pl.pallas_call(fourier_kernel, name='fourier', out_shape=(jax.ShapeDtypeS...  2.89 us

profile of v4, /device:TPU:1, one launch (start us, length us, event | category | flops | bytes accessed | tf_op | source)
XLA Modules:
  0.0 58.3 jit_solution(3107077891630699704)
XLA Ops:
  0.6 0.0 copy-start.1
  0.6 0.0 copy-start
  0.7 2.9 %fourier.1 = (bf16[16,32,128]{2,1,0:T(8,128)(2,1)S(1)}, s32[8,128]{1,0:T(8,128)S(1)}) custom-call(s32[16]{0:T(128)} %wlist_hbm.1, s32[1,80]{1,0:T(1,128)} %bitcast.12, bf16[4,2,80,2560]{3,2,1,0:T(8,128)(2,1)} %grid_hbm.1), custom_call_target="tpu_custom_call" | custom-call | tf_op jit(solution)/shard_map/fourier/pallas_call | solution.py:188
  3.6 17.3 %all_to_all.15.rows_ref = bf16[16,32,128]{2,1,0:T(8,128)(2,1)S(1)} all-to-all(bf16[16,32,128]{2,1,0:T(8,128)(2,1)S(1)} %get-tuple-element.12), channel_id=1, replica_groups={{416,448,480,0,32,64,96,128,160,192,224,256,288,320,352,384},{417,449,4..., dimensions={0} | all-to-all | bytes 262144 | tf_op jit(solution)/shard_map/all_to_all | solution.py:264
  20.9 0.0 copy-done.1
  20.9 0.0 copy-done
  20.9 0.7 %legendre.1 = (bf16[16,88,128]{2,1,0:T(8,128)(2,1)S(1)}, f32[16,641]{1,0:T(8,128)S(1)}, f32[16,640]{1,0:T(8,128)S(1)}) custom-call(s32[8,128]{1,0:T(8,128)S(1)} %get-tuple-element.11.own_ref, bf16[16,32,128]{2,1,0:T(8,128)(2,1)S(1)} %all_to_all.15.rows_ref, bf16[1,641,640]{2,1,0:T(8,128)(2,1)S(1)} %bitcast.8, bf16[1,640,640]{2,1,0:T(8,128)(2,1)S(1)} %copy-done.1), custom_call_target="tpu_custom_call" | custom-call | tf_op jit(solution)/shard_map/legendre/pallas_call | solution.py:213
  21.6 20.3 %all_to_all.16 = bf16[32,11,4,128]{3,2,1,0:T(4,128)(2,1)S(1)} all-to-all(bf16[32,11,4,128]{3,2,1,0:T(4,128)(2,1)S(1)} %bitcast.9), channel_id=1, replica_groups={{22,23,16,17,18,19,20,21,30,31,24,25,26,27,28,29,6,7,0,1,2,3,4,5,14,15,..., dimensions={0} | all-to-all | bytes 720896 | tf_op jit(solution)/shard_map/all_to_all | solution.py:272
  41.9 0.3 gram.1
  42.2 15.5 %all_to_all.17 = bf16[64,4,128]{2,1,0:T(4,128)(2,1)S(1)} all-to-all(bf16[64,4,128]{2,1,0:T(4,128)(2,1)S(1)} %bitcast.11), channel_id=1, replica_groups={{432,440,416,424,464,472,448,456,496,504,480,488,16,24,0,8,48,56,32,40,..., dimensions={0} | all-to-all | bytes 131072 | tf_op jit(solution)/shard_map/all_to_all | solution.py:276
  57.7 0.7 %finish.1 = (f32[4,128]{1,0:T(4,128)}, f32[1,4,2,2,641]{4,3,2,1,0:T(2,128)}, f32[1,4,2,2,640]{4,3,2,1,0:T(2,128)}) custom-call(bf16[32,8,128]{2,1,0:T(8,128)(2,1)S(1)} %bitcast.10, f32[16,641]{1,0:T(8,128)S(1)} %get-tuple-element.14.even_in_ref, f32[16,640]{1,0:T(8,128)S(1)} %get-tuple-element.15.odd_in_ref), custom_call_target="tpu_custom_call" | custom-call | tf_op jit(solution)/shard_map/finish/pallas_call | solution.py:243
Async XLA Ops:
  0.6 20.3 %copy-start.1 = (bf16[1,640,640]{2,1,0:T(8,128)(2,1)S(1)}, bf16[1,640,640]{2,1,0:T(8,128)(2,1)}, u32[]{:S(2)}) copy-start(bf16[1,640,640]{2,1,0:T(8,128)(2,1)} %odd_ref.1) | copy-start | bytes 2457604
  0.6 20.2 %copy-start = (bf16[1,640,641]{1,2,0:T(8,128)(2,1)S(1)}, bf16[1,640,641]{1,2,0:T(8,128)(2,1)}, u32[]{:S(2)}) copy-start(bf16[1,640,641]{1,2,0:T(8,128)(2,1)} %param.8) | copy-start | bytes 2461444

commit v5 on v4

--- a/solution.py
+++ b/solution.py
@@ -9,18 +9,19 @@
 from jax.sharding import PartitionSpec as P
 
 F32 = jnp.float32
-FIRST_BAND, FIRST_X, FIRST_Z = 13, 2, 6
+FOURIER_BANDS = [11, 12, 13, 14, 15, 0, 1, 2, 3, 4, 5, 6, 7, 8, 9, 10]
+TILE_PAIRS = [
+    (2, 3), (1, 3), (3, 3), (0, 3), (2, 0), (2, 2), (1, 0), (1, 2),
+    (3, 0), (3, 2), (0, 0), (0, 2), (2, 1), (1, 1), (3, 1), (0, 1),
+]
+PRODUCT_BANDS = [11, 2, 3, 0, 4, 1, 5, 6, 14, 7, 15, 8, 12, 9, 13, 10]
+PRODUCT_XS = [2, 0, 1, 3]
 BF16 = jnp.bfloat16
 NT = (((1,), (1,)), ((), ()))
 NN = (((1,), (0,)), ((), ()))
 
 
-def turned(count, first):
-    return [(first + n) % count for n in range(count)]
-
-
-def fourier_kernel(wlist_hbm, trunc_hbm, grid_hbm, out_ref, own_ref, wlist_ref, trunc_ref, grid_ref, table, rows, small, sems):
-    vectors, fields, lats, lons = grid_ref.shape
+def table_kernel(lats, lons, wlist_hbm, trunc_hbm, table, keep_ref, own_ref, wlist_ref, trunc_ref, small):
     bands = wlist_ref.shape[0]
     total_lat = lats * bands
     members = 2 * bands
@@ -28,19 +29,12 @@
     get_trunc = pltpu.make_async_copy(trunc_hbm, trunc_ref, small.at[1])
     get_wlist.start()
     get_trunc.start()
-    half = vectors // 2
-    fetches = [
-        pltpu.make_async_copy(grid_hbm.at[pl.ds(v, half)], grid_ref.at[pl.ds(v, half)], sems.at[n])
-        for n, v in enumerate(range(0, vectors, half))
-    ]
-    for fetch in fetches:
-        fetch.start()
     row = lax.broadcasted_iota(jnp.int32, (members, 128), 0)
     lane = lax.broadcasted_iota(jnp.int32, (members, 128), 1)
     get_wlist.wait()
     mvals = jnp.zeros((members, 128), jnp.int32)
     for b in range(bands):
-        wave, place = wlist_ref[b], (b - FIRST_BAND) % bands
+        wave, place = wlist_ref[b], FOURIER_BANDS.index(b)
         mvals = jnp.where(row == place, wave, mvals)
         mvals = jnp.where(row == bands + place, total_lat - 1 - wave, mvals)
     own_ref[...] = jnp.full(own_ref.shape, wlist_ref[lax.axis_index("band")], jnp.int32)
@@ -57,38 +51,68 @@
         table[members:, 128 * i : 128 * (i + 1)] = (-(cs * fine_cos + cc * fine_sin)).astype(BF16)
     get_trunc.wait()
     keep = mvals[:, :lats] <= trunc_ref[...]
-    keep = jnp.concatenate([keep, keep], axis=0)
-    depth = 4 * vectors * fields
+    keep = jnp.where(keep, 1.0, 0.0)
+    keep_ref[...] = jnp.concatenate([keep, keep], axis=0)
+
+
+def pack_kernel(spectra_ref, keep_ref, out_ref, rows):
+    bands = out_ref.shape[0]
+    lats = keep_ref.shape[1]
+    fields, vectors = 2, spectra_ref.shape[1] // (2 * lats)
+    keep = keep_ref[...] > 0
+    depth = out_ref.shape[1]
+    wide = lax.broadcasted_iota(jnp.int32, (bands, 128), 1)
     for v in range(vectors):
-        if v % half == 0:
-            fetches[v // half].wait()
+        fields_of = []
         for f in range(fields):
-            spectra = lax.dot_general(table[...], grid_ref[v, f], NT, preferred_element_type=F32)
+            place = lats * (v * fields + f)
+            spectra = spectra_ref[:, place : place + lats]
             spectra = jnp.where(keep, spectra, 0.0)
-            spectra = jnp.pad(spectra, ((0, 0), (0, 128 - lats)))
-            for r in range(2):
-                for p in range(2):
-                    place = ((p * fields + f) * 2 + r) * vectors + v
-                    start = (r * 2 + p) * bands
-                    rows[pl.ds(place, bands, stride=depth), :] = spectra[start : start + bands]
+            fields_of.append(jnp.pad(spectra, ((0, 0), (0, 128 - lats))))
+        for r in range(2):
+            others = jnp.zeros((bands, 128), F32)
+            for p in range(2):
+                start = (r * 2 + p) * bands
+                one, two = (spectra[start : start + bands] for spectra in fields_of)
+                rows[pl.ds((p * 2 + r) * vectors + v, bands, stride=depth), :] = jnp.where(
+                    wide < 64, one, pltpu.roll(two, 64, 1)
+                )
+                for f, spectra in enumerate((one, two)):
+                    place = 16 * (p * fields + f)
+                    mine = (wide >= place) & (wide < place + 16)
+                    others = jnp.where(mine, pltpu.roll(spectra, (place + 64) % 128, 1), others)
+            rows[pl.ds((4 + r) * vectors + v, bands, stride=depth), :] = others
     out_ref[...] = rows[...].astype(BF16).reshape(out_ref.shape)
 
 
 def legendre_kernel(own_ref, rows_ref, even_t_ref, odd_ref, send_ref, even_ref, odd_out_ref, fold):
-    bands, depth, _ = rows_ref.shape
+    bands = rows_ref.shape[0]
     half_bands = bands // 2
     hemisphere = odd_ref.shape[1]
     lats = hemisphere // half_bands
     total_lat = 2 * hemisphere
+    depth = fold.shape[1]
     own = own_ref[0:1, 0:1]
+
+    def slab(band):
+        packed = rows_ref[FOURIER_BANDS.index(band)].astype(F32)
+        others = packed[2 * depth // 4 :]
+        groups = []
+        for p in range(2):
+            for f in range(2):
+                main = packed[p * depth // 4 : (p + 1) * depth // 4]
+                main = pltpu.roll(main, 64, 1) if f else main
+                groups.append(jnp.where(low, main, pltpu.roll(others, 64 - 16 * (p * 2 + f), 1)))
+        return jnp.concatenate(groups, axis=0)
+
     ri = lax.broadcasted_iota(jnp.int32, (128, 128), 0)
     ci = lax.broadcasted_iota(jnp.int32, (128, 128), 1)
+    low = ci[: depth // 4] < 64
     mirror = jnp.where(ri + ci == lats - 1, 1.0, 0.0).astype(BF16)
-    south = [rows_ref[(b - FIRST_BAND) % bands] for b in range(half_bands, bands)]
-    south = jnp.concatenate(south, axis=0)
+    south = jnp.concatenate([slab(b) for b in range(half_bands, bands)], axis=0).astype(BF16)
     south = lax.dot_general(south, mirror, NN, preferred_element_type=F32)
     for b in range(half_bands):
-        north_b = rows_ref[(b - FIRST_BAND) % bands].astype(F32)
+        north_b = slab(b)
         s = half_bands - 1 - b
         south_b = south[s * depth : (s + 1) * depth]
         fold[0, :, lats * b : lats * (b + 1)] = (north_b + south_b)[:, :lats]
@@ -121,8 +145,9 @@
         quarters = 2 * list(range(len(pieces)))
         slab = [jnp.where(first, low[i], high[j]) for i, j in zip(quarters[0::2], quarters[1::2])]
         slab = jnp.concatenate(slab, axis=0).astype(BF16)
-        for pair in range(columns // 2):
-            send_ref[fr * columns // 2 + pair] = slab
+        for place, (x, _) in enumerate(TILE_PAIRS):
+            if x == fr:
+                send_ref[place] = slab
 
 
 def gram_kernel(columns, tiles_ref, out_ref, gram_ref):
@@ -131,10 +156,7 @@
     count, tiles = 2 * pairs, depth // (2 * vectors)
     wide = count // columns
     half_z = columns // 2
-    half_first = FIRST_Z // 2
-    places = [
-        (x - FIRST_X) % wide * half_z + (z - half_first) % half_z for x in range(wide) for z in range(half_z)
-    ]
+    places = [TILE_PAIRS.index((x, z)) for x in range(wide) for z in range(columns // 2)]
     slabs = jnp.stack([tiles_ref[n] for n in places]).astype(F32)
     eights = [slabs[:, 8 * k : 8 * (k + 1)] for k in range(tiles)]
     first = lax.broadcasted_iota(jnp.int32, (pairs, 8, 128), 1) < vectors
@@ -151,7 +173,7 @@
     gram = lax.dot_general(both, both, NT, preferred_element_type=F32)
     gram_ref[...] = gram.reshape(gram_ref.shape)
     z = lax.axis_index("z")
-    rows = [gram_ref[(x + FIRST_X) % wide, lax.div(z, 2)] for x in range(wide)]
+    rows = [gram_ref[x, lax.div(z, 2)] for x in PRODUCT_XS]
     rows = [jnp.where(lax.rem(z, 2) == 0, row, pltpu.roll(row, vectors, 0)) for row in rows]
     first = lax.broadcasted_iota(jnp.int32, (8, 128), 0) < vectors
     rows = [jnp.where(first, rows[x], pltpu.roll(rows[x + 1], vectors, 0)) for x in range(0, wide, 2)]
@@ -184,31 +206,39 @@
 def fourier(wlist, trunc, grid):
     vectors, fields, lats, lons = grid.shape
     bands = wlist.shape[0]
-    depth = 4 * vectors * fields
-    return pl.pallas_call(
-        fourier_kernel,
-        name="fourier",
+    depth = 6 * vectors
+    table, keep, own = pl.pallas_call(
+        functools.partial(table_kernel, lats, lons),
+        name="table",
         out_shape=(
-            jax.ShapeDtypeStruct((bands, depth, 128), BF16),
+            jax.ShapeDtypeStruct((4 * bands, lons), BF16),
+            jax.ShapeDtypeStruct((4 * bands, lats), F32),
             jax.ShapeDtypeStruct((8, 128), jnp.int32),
         ),
-        in_specs=[HBM, HBM, HBM],
-        out_specs=(VMEM, VMEM),
+        in_specs=[HBM, HBM],
+        out_specs=(VMEM, VMEM, VMEM),
         scratch_shapes=[
             pltpu.SMEM((bands,), jnp.int32),
             pltpu.VMEM((1, lats), jnp.int32),
-            pltpu.VMEM(grid.shape, BF16),
-            pltpu.VMEM((4 * bands, lons), BF16),
-            pltpu.VMEM((bands * depth, 128), F32),
-            pltpu.SemaphoreType.DMA((2,)),
             pltpu.SemaphoreType.DMA((2,)),
         ],
         compiler_params=PARAMS,
-    )(in_hbm(wlist), in_hbm(trunc.reshape(1, lats)), in_hbm(grid))
+    )(in_hbm(wlist), in_hbm(trunc.reshape(1, lats)))
+    spectra = lax.dot_general(table, grid.reshape(-1, lons), NT, preferred_element_type=F32)
+    lat_rows = pl.pallas_call(
+        pack_kernel,
+        name="pack",
+        out_shape=jax.ShapeDtypeStruct((bands, depth, 128), BF16),
+        in_specs=[VMEM, VMEM],
+        out_specs=VMEM,
+        scratch_shapes=[pltpu.VMEM((bands * depth, 128), F32)],
+        compiler_params=PARAMS,
+    )(spectra, keep)
+    return lat_rows, own
 
 
 def legendre(own, received, leg_even, leg_odd, vectors, tans):
-    depth = received.shape[1]
+    depth = 8 * vectors
     hemisphere = leg_odd.shape[2]
     return pl.pallas_call(
         legendre_kernel,
@@ -262,17 +292,17 @@
     total_lat = lats * bands
     lat_rows, own = fourier(wlist, trunc, grid)
     received = lax.all_to_all(
-        lat_rows, "band", 0, 0, axis_index_groups=[turned(bands, FIRST_BAND)], tiled=True
+        lat_rows, "band", 0, 0, axis_index_groups=[FOURIER_BANDS], tiled=True
     )
     tiles, even, odd = legendre(own, received, leg_even, leg_odd, vectors, tans)
     slab = tiles.shape
     tiles = tiles.reshape(tans, slab[1] // (2 * vectors), vectors, 128)
     wide = tans // columns
-    tan_group = [x * columns + z for x in turned(wide, FIRST_X) for z in turned(columns, FIRST_Z)]
+    tan_group = [x * columns + 2 * z + n for x, z in TILE_PAIRS for n in range(2)]
     tiles = lax.all_to_all(tiles, ("x", "z"), 0, 0, axis_index_groups=[tan_group], tiled=True)
     products = gram(tiles.reshape(slab), columns, bands, vectors)
     products = products.reshape(-1, vectors, vectors * tans)
-    group = [b * wide + x for b in turned(bands, FIRST_BAND) for x in turned(wide, FIRST_X)]
+    group = [b * wide + x for b in PRODUCT_BANDS for x in PRODUCT_XS]
     products = lax.all_to_all(products, ("band", "x"), 0, 0, axis_index_groups=[group], tiled=True)
     products = products.reshape(-1, 2 * vectors, vectors * tans)
     scale = 1.0 / (bands * 4.0 * (total_lat + 1))

time: 58.5 us -> 56.9 us (0.973)
  blocking collectives: 53.1 us -> 50.9 us
  Pallas kernels: 4.54 us -> 3.27 us
  matrix products: 0 us -> 1.1 us
  local copies, waits for them, and re-layouts: 0.01 us -> 0.75 us
    all_to_all x1, blocking collectives: 15.5 us -> 14 us  [on_device(): lax.all_to_all(products, ('band', 'x'), 0, 0, axis_index_groups=[group],...]
    pallas_call x1 -> x2, Pallas kernels: 2.89 us -> 1.53 us  [the longest x1 1.17 us: fourier(): pl.pallas_call(functools.partial(table_kernel, lats, lons), name='table',...]
    dot_general x0 -> x1, matrix products: none -> 1.1 us  [fourier(): lax.dot_general(table, grid.reshape(-1, lons), NT, preferred_element_type...]
    unnamed x4 -> x6, local copies, waits for them, and re-layouts: 0.01 us -> 0.75 us
where the time goes in v5:
time: 56.9 us; the launch traced here: 56.7 us
  blocking collectives  50.9 us (89%)
  Pallas kernels  3.27 us (6%)
  matrix products  1.1 us (2%)
  local copies, waits for them, and re-layouts  0.75 us (1%)
  between operations  0.7 us (1%)
    all_to_all x1, blocking collectives, on_device(): lax.all_to_all(tiles, ('x', 'z'), 0, 0, axis_index_groups=[tan_group], ti...  20.1 us
    all_to_all x1, blocking collectives, on_device(): lax.all_to_all(lat_rows, 'band', 0, 0, axis_index_groups=[FOURIER_BANDS],...  16.8 us
    all_to_all x1, blocking collectives, on_device(): lax.all_to_all(products, ('band', 'x'), 0, 0, axis_index_groups=[group],...  14 us
    pallas_call x1, Pallas kernels, fourier(): pl.pallas_call(functools.partial(table_kernel, lats, lons), name='table',...  1.17 us

profile of v5, /device:TPU:1, one launch (start us, length us, event | category | flops | bytes accessed | tf_op | source)
XLA Modules:
  0.0 56.7 jit_solution(16766954320713443826)
XLA Ops:
  0.6 0.0 copy-start
  0.6 0.0 copy-start.2
  0.7 0.0 copy-start.1
  0.7 1.2 %table.1 = (bf16[64,2560]{1,0:T(8,128)(2,1)S(1)}, f32[64,80]{1,0:T(8,128)S(1)}, s32[8,128]{1,0:T(8,128)S(1)}) custom-call(s32[16]{0:T(128)} %wlist_hbm.1, s32[1,80]{1,0:T(1,128)} %bitcast.17), custom_call_target="tpu_custom_call" | custom-call | tf_op jit(solution)/shard_map/table/pallas_call | solution.py:210
  1.8 0.7 %copy-done = bf16[4,2,80,2560]{3,2,1,0:T(8,128)(2,1)S(1)} copy-done((bf16[4,2,80,2560]{3,2,1,0:T(8,128)(2,1)S(1)}, bf16[4,2,80,2560]{3,2,1,0:T(8,128)(2,1)}, u32[]{:S(2)}) %copy-start) | copy-done | bytes 3276824
  2.6 1.1 %fusion.spectra_ref = f32[64,640]{1,0:T(8,128)S(1)} fusion(bf16[64,2560]{1,0:T(8,128)(2,1)S(1)} %get-tuple-element.13, bf16[640,2560]{1,0:T(8,128)(2,1)S(1)} %bitcast.10), kind=kOutput, calls=%fused_computation | convolution fusion | flops 209715200 | bytes 3768320 | tf_op jit(solution)/shard_map/dot_general | solution.py:227
  3.7 0.4 pack.1
  4.1 16.8 %all_to_all.15.rows_ref = bf16[16,24,128]{2,1,0:T(8,128)(2,1)S(1)} all-to-all(bf16[16,24,128]{2,1,0:T(8,128)(2,1)S(1)} %pack.1), channel_id=1, replica_groups={{352,384,416,448,480,0,32,64,96,128,160,192,224,256,288,320},{353,385,4..., dimensions={0} | all-to-all | bytes 196608 | tf_op jit(solution)/shard_map/all_to_all | solution.py:294
  20.9 0.0 copy-done.2
  20.9 0.0 copy-done.1
  20.9 0.8 %legendre.1 = (bf16[16,88,128]{2,1,0:T(8,128)(2,1)S(1)}, f32[16,641]{1,0:T(8,128)S(1)}, f32[16,640]{1,0:T(8,128)S(1)}) custom-call(s32[8,128]{1,0:T(8,128)S(1)} %get-tuple-element.12.own_ref, bf16[16,24,128]{2,1,0:T(8,128)(2,1)S(1)} %all_to_all.15.rows_ref, bf16[1,641,640]{2,1,0:T(8,128)(2,1)S(1)} %bitcast.12, bf16[1,640,640]{2,1,0:T(8,128)(2,1)S(1)} %copy-done.2), custom_call_target="tpu_custom_call" | custom-call | tf_op jit(solution)/shard_map/legendre/pallas_call | solution.py:243
  21.7 20.1 %all_to_all.16 = bf16[32,11,4,128]{3,2,1,0:T(4,128)(2,1)S(1)} all-to-all(bf16[32,11,4,128]{3,2,1,0:T(4,128)(2,1)S(1)} %bitcast.13), channel_id=1, replica_groups={{22,23,14,15,30,31,6,7,16,17,20,21,8,9,12,13,24,25,28,29,0,1,4,5,18,19,..., dimensions={0} | all-to-all | bytes 720896 | tf_op jit(solution)/shard_map/all_to_all | solution.py:302
  41.7 0.3 gram.1
  42.0 14.0 %all_to_all.17 = bf16[64,4,128]{2,1,0:T(4,128)(2,1)S(1)} all-to-all(bf16[64,4,128]{2,1,0:T(4,128)(2,1)S(1)} %bitcast.15), channel_id=1, replica_groups={{368,352,360,376,80,64,72,88,112,96,104,120,16,0,8,24,144,128,136,152,4..., dimensions={0} | all-to-all | bytes 131072 | tf_op jit(solution)/shard_map/all_to_all | solution.py:306
  56.1 0.7 %finish.1 = (f32[4,128]{1,0:T(4,128)}, f32[1,4,2,2,641]{4,3,2,1,0:T(2,128)}, f32[1,4,2,2,640]{4,3,2,1,0:T(2,128)}) custom-call(bf16[32,8,128]{2,1,0:T(8,128)(2,1)S(1)} %bitcast.14, f32[16,641]{1,0:T(8,128)S(1)} %get-tuple-element.16.even_in_ref, f32[16,640]{1,0:T(8,128)S(1)} %get-tuple-element.17.odd_in_ref), custom_call_target="tpu_custom_call" | custom-call | tf_op jit(solution)/shard_map/finish/pallas_call | solution.py:273
Async XLA Ops:
  0.6 1.9 %copy-start = (bf16[4,2,80,2560]{3,2,1,0:T(8,128)(2,1)S(1)}, bf16[4,2,80,2560]{3,2,1,0:T(8,128)(2,1)}, u32[]{:S(2)}) copy-start(bf16[4,2,80,2560]{3,2,1,0:T(8,128)(2,1)} %param.5) | copy-start | bytes 9830404
  0.6 20.2 %copy-start.2 = (bf16[1,640,640]{2,1,0:T(8,128)(2,1)S(1)}, bf16[1,640,640]{2,1,0:T(8,128)(2,1)}, u32[]{:S(2)}) copy-start(bf16[1,640,640]{2,1,0:T(8,128)(2,1)} %odd_ref.1) | copy-start | bytes 2457604
  0.7 20.2 %copy-start.1 = (bf16[1,640,641]{1,2,0:T(8,128)(2,1)S(1)}, bf16[1,640,641]{1,2,0:T(8,128)(2,1)}, u32[]{:S(2)}) copy-start(bf16[1,640,641]{1,2,0:T(8,128)(2,1)} %param.8) | copy-start | bytes 2461444

commit v6 on v5

--- a/solution.py
+++ b/solution.py
@@ -133,53 +133,41 @@
     columns = 2 * send_ref.shape[0] // parts
     last = jnp.broadcast_to(even[:, hemisphere : hemisphere + 1], (half, 128))
     last = jnp.where(lax.broadcasted_iota(jnp.int32, (half, 128), 1) == 0, last, 0.0)
-    pieces = [even[:, 128 * i : 128 * (i + 1)] for i in range(tiles)]
-    pieces += [odd[:, 128 * i : 128 * (i + 1)] for i in range(tiles)]
-    pieces += [last]
+    pieces = [even[:, 128 * i : 128 * (i + 1)] for i in range(tiles)] + [last]
+    pieces += [odd[:, 128 * i : 128 * (i + 1)] for i in range(tiles)] + [jnp.zeros_like(last)]
     first = lax.broadcasted_iota(jnp.int32, (8, 128), 0) < vectors
     for fr in range(parts):
         base = fr // 2 * 8
         same = [piece[base : base + 8] for piece in pieces]
         other = [pltpu.roll(piece, vectors, 0) for piece in same]
         low, high = (same, other) if fr % 2 == 0 else (other, same)
-        quarters = 2 * list(range(len(pieces)))
-        slab = [jnp.where(first, low[i], high[j]) for i, j in zip(quarters[0::2], quarters[1::2])]
-        slab = jnp.concatenate(slab, axis=0).astype(BF16)
+        eights = [jnp.where(first, low[i], high[i + 1]) for i in range(0, len(pieces), 2)]
+        block = jnp.concatenate(eights, axis=0).astype(BF16)
         for place, (x, _) in enumerate(TILE_PAIRS):
             if x == fr:
-                send_ref[place] = slab
+                send_ref[place] = block
 
 
 def gram_kernel(columns, tiles_ref, out_ref, gram_ref):
     pairs, depth, _ = tiles_ref.shape
-    vectors = 4
-    count, tiles = 2 * pairs, depth // (2 * vectors)
-    wide = count // columns
-    half_z = columns // 2
+    wide = pairs // (columns // 2)
     places = [TILE_PAIRS.index((x, z)) for x in range(wide) for z in range(columns // 2)]
     slabs = jnp.stack([tiles_ref[n] for n in places]).astype(F32)
-    eights = [slabs[:, 8 * k : 8 * (k + 1)] for k in range(tiles)]
-    first = lax.broadcasted_iota(jnp.int32, (pairs, 8, 128), 1) < vectors
-    half = tiles // 2
-    columns_of = []
-    for i in range(tiles):
-        if i % 2 == 0:
-            both = jnp.where(first, eights[i // 2], eights[half + i // 2])
-        else:
-            both = jnp.where(first, eights[half + (i + 1) // 2], eights[i // 2])
-            both = pltpu.roll(both, vectors, 1)
-        columns_of.append(both.reshape(count * vectors, 128).astype(BF16))
-    both = jnp.concatenate(columns_of, axis=1)
+    eights = [slabs[:, 8 * k : 8 * (k + 1)] for k in range(depth // 8)]
+    half = len(eights) // 2
+    first = lax.broadcasted_iota(jnp.int32, (pairs, 8, 128), 1) < 4
+    quarters = []
+    for one, two in zip(eights[:half], eights[half:]):
+        quarters.append(jnp.where(first, one, pltpu.roll(two, 4, 1)))
+        quarters.append(jnp.where(first, pltpu.roll(one, 4, 1), two))
+    both = [quarter.reshape(8 * pairs, 128).astype(BF16) for quarter in quarters]
+    both = jnp.concatenate(both, axis=1)
     gram = lax.dot_general(both, both, NT, preferred_element_type=F32)
     gram_ref[...] = gram.reshape(gram_ref.shape)
-    z = lax.axis_index("z")
-    rows = [gram_ref[x, lax.div(z, 2)] for x in PRODUCT_XS]
-    rows = [jnp.where(lax.rem(z, 2) == 0, row, pltpu.roll(row, vectors, 0)) for row in rows]
-    first = lax.broadcasted_iota(jnp.int32, (8, 128), 0) < vectors
-    rows = [jnp.where(first, rows[x], pltpu.roll(rows[x + 1], vectors, 0)) for x in range(0, wide, 2)]
-    block = jnp.concatenate(rows, axis=0).astype(BF16)
-    for b in range(out_ref.shape[0]):
-        out_ref[b] = block
+    own = lax.div(lax.axis_index("z"), 2)
+    blocks = [gram_ref[x, own].astype(BF16) for x in PRODUCT_XS]
+    for n in range(out_ref.shape[0]):
+        out_ref[n] = blocks[n % wide]
 
 
 def finish_kernel(scale, parts_ref, even_in_ref, odd_in_ref, inner_ref, even_ref, odd_ref):
@@ -244,7 +232,7 @@
         legendre_kernel,
         name="legendre",
         out_shape=(
-            jax.ShapeDtypeStruct((tans // 2, 2 * (hemisphere // 64 + 1) * vectors, 128), BF16),
+            jax.ShapeDtypeStruct((tans // 2, 2 * (hemisphere // 128 + 1) * vectors, 128), BF16),
             jax.ShapeDtypeStruct((depth // 2, leg_even.shape[2]), F32),
             jax.ShapeDtypeStruct((depth // 2, leg_odd.shape[2]), F32),
         ),
@@ -261,7 +249,7 @@
     return pl.pallas_call(
         functools.partial(gram_kernel, columns),
         name="gram",
-        out_shape=jax.ShapeDtypeStruct((bands, wide * vectors, vectors * tans), BF16),
+        out_shape=jax.ShapeDtypeStruct((bands * wide, 2 * vectors, vectors * tans), BF16),
         in_specs=[VMEM],
         out_specs=VMEM,
         scratch_shapes=[pltpu.VMEM((wide, columns // 2, 2 * vectors, vectors * tans), F32)],
@@ -296,14 +284,17 @@
     )
     tiles, even, odd = legendre(own, received, leg_even, leg_odd, vectors, tans)
     slab = tiles.shape
-    tiles = tiles.reshape(tans, slab[1] // (2 * vectors), vectors, 128)
+    tiles = tiles.reshape(tans, slab[1] // 4, 2, 128)
     wide = tans // columns
     tan_group = [x * columns + 2 * z + n for x, z in TILE_PAIRS for n in range(2)]
     tiles = lax.all_to_all(tiles, ("x", "z"), 0, 0, axis_index_groups=[tan_group], tiled=True)
     products = gram(tiles.reshape(slab), columns, bands, vectors)
     products = products.reshape(-1, vectors, vectors * tans)
-    group = [b * wide + x for b in PRODUCT_BANDS for x in PRODUCT_XS]
-    products = lax.all_to_all(products, ("band", "x"), 0, 0, axis_index_groups=[group], tiled=True)
+    product_groups = [
+        [(b * wide + x) * columns + z + n for b in PRODUCT_BANDS for x in PRODUCT_XS for n in range(2)]
+        for z in range(0, columns, 2)
+    ]
+    products = lax.all_to_all(products, ("band", "x", "z"), 0, 0, axis_index_groups=product_groups, tiled=True)
     products = products.reshape(-1, 2 * vectors, vectors * tans)
     scale = 1.0 / (bands * 4.0 * (total_lat + 1))
     inner, even, odd = finish(products, even, odd, scale, vectors, fields)

time: 56.9 us -> 56.2 us (0.988)
  blocking collectives: 50.9 us -> 50.3 us
    all_to_all x1, blocking collectives: 20.1 us -> 16.7 us  [on_device(): lax.all_to_all(tiles, ('x', 'z'), 0, 0, axis_index_groups=[tan_group], ti...]
    all_to_all x1, blocking collectives: 14 us -> 16.8 us  [on_device(): lax.all_to_all(products, ('band', 'x', 'z'), 0, 0, axis_index_groups=prod...]
where the time goes in v6:
time: 56.2 us; the launch traced here: 56 us
  blocking collectives  50.3 us (90%)
  Pallas kernels  3.22 us (6%)
  matrix products  1.1 us (2%)
  local copies, waits for them, and re-layouts  0.75 us (1%)
  between operations  0.7 us (1%)
    all_to_all x1, blocking collectives, on_device(): lax.all_to_all(lat_rows, 'band', 0, 0, axis_index_groups=[FOURIER_BANDS],...  16.8 us
    all_to_all x1, blocking collectives, on_device(): lax.all_to_all(products, ('band', 'x', 'z'), 0, 0, axis_index_groups=prod...  16.8 us
    all_to_all x1, blocking collectives, on_device(): lax.all_to_all(tiles, ('x', 'z'), 0, 0, axis_index_groups=[tan_group], ti...  16.7 us
    pallas_call x1, Pallas kernels, fourier(): pl.pallas_call(functools.partial(table_kernel, lats, lons), name='table',...  1.17 us

profile of v6, /device:TPU:1, one launch (start us, length us, event | category | flops | bytes accessed | tf_op | source)
XLA Modules:
  0.0 56.0 jit_solution(14604728551503332039)
XLA Ops:
  0.6 0.0 copy-start
  0.6 0.0 copy-start.2
  0.7 0.0 copy-start.1
  0.7 1.2 %table.1 = (bf16[64,2560]{1,0:T(8,128)(2,1)S(1)}, f32[64,80]{1,0:T(8,128)S(1)}, s32[8,128]{1,0:T(8,128)S(1)}) custom-call(s32[16]{0:T(128)} %wlist_hbm.1, s32[1,80]{1,0:T(1,128)} %bitcast.17), custom_call_target="tpu_custom_call" | custom-call | tf_op jit(solution)/shard_map/table/pallas_call | solution.py:198
  1.8 0.7 %copy-done = bf16[4,2,80,2560]{3,2,1,0:T(8,128)(2,1)S(1)} copy-done((bf16[4,2,80,2560]{3,2,1,0:T(8,128)(2,1)S(1)}, bf16[4,2,80,2560]{3,2,1,0:T(8,128)(2,1)}, u32[]{:S(2)}) %copy-start) | copy-done | bytes 3276824
  2.6 1.1 %fusion.spectra_ref = f32[64,640]{1,0:T(8,128)S(1)} fusion(bf16[64,2560]{1,0:T(8,128)(2,1)S(1)} %get-tuple-element.13, bf16[640,2560]{1,0:T(8,128)(2,1)S(1)} %bitcast.10), kind=kOutput, calls=%fused_computation | convolution fusion | flops 209715200 | bytes 3768320 | tf_op jit(solution)/shard_map/dot_general | solution.py:215
  3.7 0.4 pack.1
  4.1 16.8 %all_to_all.15.rows_ref = bf16[16,24,128]{2,1,0:T(8,128)(2,1)S(1)} all-to-all(bf16[16,24,128]{2,1,0:T(8,128)(2,1)S(1)} %pack.1), channel_id=1, replica_groups={{352,384,416,448,480,0,32,64,96,128,160,192,224,256,288,320},{353,385,4..., dimensions={0} | all-to-all | bytes 196608 | tf_op jit(solution)/shard_map/all_to_all | solution.py:282
  20.9 0.0 copy-done.2
  20.9 0.0 copy-done.1
  20.9 0.8 %legendre.1 = (bf16[16,48,128]{2,1,0:T(8,128)(2,1)S(1)}, f32[16,641]{1,0:T(8,128)S(1)}, f32[16,640]{1,0:T(8,128)S(1)}) custom-call(s32[8,128]{1,0:T(8,128)S(1)} %get-tuple-element.12.own_ref, bf16[16,24,128]{2,1,0:T(8,128)(2,1)S(1)} %all_to_all.15.rows_ref, bf16[1,641,640]{2,1,0:T(8,128)(2,1)S(1)} %bitcast.11, bf16[1,640,640]{2,1,0:T(8,128)(2,1)S(1)} %copy-done.2), custom_call_target="tpu_custom_call" | custom-call | tf_op jit(solution)/shard_map/legendre/pallas_call | solution.py:231
  21.7 16.7 %all_to_all.16 = bf16[32,12,2,128]{3,2,1,0:T(2,128)(2,1)S(1)} all-to-all(bf16[32,12,2,128]{3,2,1,0:T(2,128)(2,1)S(1)} %bitcast.15), channel_id=1, replica_groups={{22,23,14,15,30,31,6,7,16,17,20,21,8,9,12,13,24,25,28,29,0,1,4,5,18,19,..., dimensions={0} | all-to-all | bytes 393216 | tf_op jit(solution)/shard_map/all_to_all | solution.py:290
  38.4 0.2 gram.1
  38.6 16.8 %all_to_all.17 = bf16[128,4,128]{2,1,0:T(4,128)(2,1)S(1)} all-to-all(bf16[128,4,128]{2,1,0:T(4,128)(2,1)S(1)} %bitcast.14), channel_id=1, replica_groups={{368,369,352,353,360,361,376,377,80,81,64,65,72,73,88,89,112,113,96,97,..., dimensions={0} | all-to-all | bytes 262144 | tf_op jit(solution)/shard_map/all_to_all | solution.py:297
  55.4 0.7 %finish.1 = (f32[4,128]{1,0:T(4,128)}, f32[1,4,2,2,641]{4,3,2,1,0:T(2,128)}, f32[1,4,2,2,640]{4,3,2,1,0:T(2,128)}) custom-call(bf16[64,8,128]{2,1,0:T(8,128)(2,1)S(1)} %bitcast.13, f32[16,641]{1,0:T(8,128)S(1)} %get-tuple-element.16.even_in_ref, f32[16,640]{1,0:T(8,128)S(1)} %get-tuple-element.17.odd_in_ref), custom_call_target="tpu_custom_call" | custom-call | tf_op jit(solution)/shard_map/finish/pallas_call | solution.py:261
Async XLA Ops:
  0.6 1.9 %copy-start = (bf16[4,2,80,2560]{3,2,1,0:T(8,128)(2,1)S(1)}, bf16[4,2,80,2560]{3,2,1,0:T(8,128)(2,1)}, u32[]{:S(2)}) copy-start(bf16[4,2,80,2560]{3,2,1,0:T(8,128)(2,1)} %param.5) | copy-start | bytes 9830404
  0.6 20.2 %copy-start.2 = (bf16[1,640,640]{2,1,0:T(8,128)(2,1)S(1)}, bf16[1,640,640]{2,1,0:T(8,128)(2,1)}, u32[]{:S(2)}) copy-start(bf16[1,640,640]{2,1,0:T(8,128)(2,1)} %odd_ref.1) | copy-start | bytes 2457604
  0.7 20.2 %copy-start.1 = (bf16[1,640,641]{1,2,0:T(8,128)(2,1)S(1)}, bf16[1,640,641]{1,2,0:T(8,128)(2,1)}, u32[]{:S(2)}) copy-start(bf16[1,640,641]{1,2,0:T(8,128)(2,1)} %param.8) | copy-start | bytes 2461444

commit v7 on v6

--- a/solution.py
+++ b/solution.py
@@ -19,6 +19,19 @@
 BF16 = jnp.bfloat16
 NT = (((1,), (1,)), ((), ()))
 NN = (((1,), (0,)), ((), ()))
+
+
+def cos_sin(phase, count):
+    phase = phase % count
+    quarter = count // 4
+    turn = (phase + quarter // 2) // quarter
+    angle = (phase - turn * quarter).astype(F32) * (2.0 * math.pi / count)
+    square = angle * angle
+    cos = 1.0 + square * (-1 / 2 + square * (1 / 24 + square * (-1 / 720 + square * (1 / 40320))))
+    sin = angle * (1.0 + square * (-1 / 6 + square * (1 / 120 + square * (-1 / 5040 + square * (1 / 362880)))))
+    odd = (turn & 1) == 1
+    cos, sin = jnp.where(odd, sin, cos), jnp.where(odd, cos, sin)
+    return jnp.where(((turn + 1) & 2) == 2, -cos, cos), jnp.where((turn & 2) == 2, -sin, sin)
 
 
 def table_kernel(lats, lons, wlist_hbm, trunc_hbm, table, keep_ref, own_ref, wlist_ref, trunc_ref, small):
@@ -38,13 +51,11 @@
         mvals = jnp.where(row == place, wave, mvals)
         mvals = jnp.where(row == bands + place, total_lat - 1 - wave, mvals)
     own_ref[...] = jnp.full(own_ref.shape, wlist_ref[lax.axis_index("band")], jnp.int32)
-    unit = 2.0 * math.pi / lons
     scaling = 1.0 / math.sqrt(lons)
     chunks = lons // 128
-    fine = (mvals * lane % lons).astype(F32) * unit
-    coarse = (mvals * lane % chunks).astype(F32) * (128.0 * unit)
-    fine_cos, fine_sin = jnp.cos(fine), jnp.sin(fine)
-    coarse_cos, coarse_sin = jnp.cos(coarse) * scaling, jnp.sin(coarse) * scaling
+    fine_cos, fine_sin = cos_sin(mvals * lane, lons)
+    coarse_cos, coarse_sin = cos_sin(mvals * lane, chunks)
+    coarse_cos, coarse_sin = coarse_cos * scaling, coarse_sin * scaling
     for i in range(chunks):
         cc, cs = coarse_cos[:, i : i + 1], coarse_sin[:, i : i + 1]
         table[:members, 128 * i : 128 * (i + 1)] = (cc * fine_cos - cs * fine_sin).astype(BF16)

time: 56.2 us -> 56.2 us (level)
  no operation moved by 1% of the time
where the time goes in v7:
time: 56.2 us; the launch traced here: 56 us
  blocking collectives  50.3 us (90%)
  Pallas kernels  3.19 us (6%)
  matrix products  1.1 us (2%)
  local copies, waits for them, and re-layouts  0.79 us (1%)
  between operations  0.7 us (1%)
    all_to_all x1, blocking collectives, on_device(): lax.all_to_all(lat_rows, 'band', 0, 0, axis_index_groups=[FOURIER_BANDS],...  16.8 us
    all_to_all x1, blocking collectives, on_device(): lax.all_to_all(products, ('band', 'x', 'z'), 0, 0, axis_index_groups=prod...  16.8 us
    all_to_all x1, blocking collectives, on_device(): lax.all_to_all(tiles, ('x', 'z'), 0, 0, axis_index_groups=[tan_group], ti...  16.7 us
    pallas_call x1, Pallas kernels, fourier(): pl.pallas_call(functools.partial(table_kernel, lats, lons), name='table',...  1.14 us

profile of v7, /device:TPU:1, one launch (start us, length us, event | category | flops | bytes accessed | tf_op | source)
XLA Modules:
  0.0 56.0 jit_solution(979894378542823068)
XLA Ops:
  0.6 0.0 copy-start
  0.6 0.0 copy-start.2
  0.7 0.0 copy-start.1
  0.7 1.1 %table.1 = (bf16[64,2560]{1,0:T(8,128)(2,1)S(1)}, f32[64,80]{1,0:T(8,128)S(1)}, s32[8,128]{1,0:T(8,128)S(1)}) custom-call(s32[16]{0:T(128)} %wlist_hbm.1, s32[1,80]{1,0:T(1,128)} %bitcast.17), custom_call_target="tpu_custom_call" | custom-call | tf_op jit(solution)/shard_map/table/pallas_call | solution.py:209
  1.8 0.8 %copy-done = bf16[4,2,80,2560]{3,2,1,0:T(8,128)(2,1)S(1)} copy-done((bf16[4,2,80,2560]{3,2,1,0:T(8,128)(2,1)S(1)}, bf16[4,2,80,2560]{3,2,1,0:T(8,128)(2,1)}, u32[]{:S(2)}) %copy-start) | copy-done | bytes 3276824
  2.6 1.1 %fusion.spectra_ref = f32[64,640]{1,0:T(8,128)S(1)} fusion(bf16[64,2560]{1,0:T(8,128)(2,1)S(1)} %get-tuple-element.13, bf16[640,2560]{1,0:T(8,128)(2,1)S(1)} %bitcast.10), kind=kOutput, calls=%fused_computation | convolution fusion | flops 209715200 | bytes 3768320 | tf_op jit(solution)/shard_map/dot_general | solution.py:226
  3.7 0.4 pack.1
  4.1 16.8 %all_to_all.15.rows_ref = bf16[16,24,128]{2,1,0:T(8,128)(2,1)S(1)} all-to-all(bf16[16,24,128]{2,1,0:T(8,128)(2,1)S(1)} %pack.1), channel_id=1, replica_groups={{352,384,416,448,480,0,32,64,96,128,160,192,224,256,288,320},{353,385,4..., dimensions={0} | all-to-all | bytes 196608 | tf_op jit(solution)/shard_map/all_to_all | solution.py:293
  20.9 0.0 copy-done.2
  20.9 0.0 copy-done.1
  20.9 0.8 %legendre.1 = (bf16[16,48,128]{2,1,0:T(8,128)(2,1)S(1)}, f32[16,641]{1,0:T(8,128)S(1)}, f32[16,640]{1,0:T(8,128)S(1)}) custom-call(s32[8,128]{1,0:T(8,128)S(1)} %get-tuple-element.12.own_ref, bf16[16,24,128]{2,1,0:T(8,128)(2,1)S(1)} %all_to_all.15.rows_ref, bf16[1,641,640]{2,1,0:T(8,128)(2,1)S(1)} %bitcast.11, bf16[1,640,640]{2,1,0:T(8,128)(2,1)S(1)} %copy-done.2), custom_call_target="tpu_custom_call" | custom-call | tf_op jit(solution)/shard_map/legendre/pallas_call | solution.py:242
  21.7 16.7 %all_to_all.16 = bf16[32,12,2,128]{3,2,1,0:T(2,128)(2,1)S(1)} all-to-all(bf16[32,12,2,128]{3,2,1,0:T(2,128)(2,1)S(1)} %bitcast.15), channel_id=1, replica_groups={{22,23,14,15,30,31,6,7,16,17,20,21,8,9,12,13,24,25,28,29,0,1,4,5,18,19,..., dimensions={0} | all-to-all | bytes 393216 | tf_op jit(solution)/shard_map/all_to_all | solution.py:301
  38.4 0.2 gram.1
  38.6 16.8 %all_to_all.17 = bf16[128,4,128]{2,1,0:T(4,128)(2,1)S(1)} all-to-all(bf16[128,4,128]{2,1,0:T(4,128)(2,1)S(1)} %bitcast.14), channel_id=1, replica_groups={{368,369,352,353,360,361,376,377,80,81,64,65,72,73,88,89,112,113,96,97,..., dimensions={0} | all-to-all | bytes 262144 | tf_op jit(solution)/shard_map/all_to_all | solution.py:308
  55.4 0.7 %finish.1 = (f32[4,128]{1,0:T(4,128)}, f32[1,4,2,2,641]{4,3,2,1,0:T(2,128)}, f32[1,4,2,2,640]{4,3,2,1,0:T(2,128)}) custom-call(bf16[64,8,128]{2,1,0:T(8,128)(2,1)S(1)} %bitcast.13, f32[16,641]{1,0:T(8,128)S(1)} %get-tuple-element.16.even_in_ref, f32[16,640]{1,0:T(8,128)S(1)} %get-tuple-element.17.odd_in_ref), custom_call_target="tpu_custom_call" | custom-call | tf_op jit(solution)/shard_map/finish/pallas_call | solution.py:272
Async XLA Ops:
  0.6 1.9 %copy-start = (bf16[4,2,80,2560]{3,2,1,0:T(8,128)(2,1)S(1)}, bf16[4,2,80,2560]{3,2,1,0:T(8,128)(2,1)}, u32[]{:S(2)}) copy-start(bf16[4,2,80,2560]{3,2,1,0:T(8,128)(2,1)} %param.5) | copy-start | bytes 9830404
  0.6 20.2 %copy-start.2 = (bf16[1,640,640]{2,1,0:T(8,128)(2,1)S(1)}, bf16[1,640,640]{2,1,0:T(8,128)(2,1)}, u32[]{:S(2)}) copy-start(bf16[1,640,640]{2,1,0:T(8,128)(2,1)} %odd_ref.1) | copy-start | bytes 2457604
  0.7 20.2 %copy-start.1 = (bf16[1,640,641]{1,2,0:T(8,128)(2,1)S(1)}, bf16[1,640,641]{1,2,0:T(8,128)(2,1)}, u32[]{:S(2)}) copy-start(bf16[1,640,641]{1,2,0:T(8,128)(2,1)} %param.8) | copy-start | bytes 2461444

commit v8 on v7

--- a/solution.py
+++ b/solution.py
@@ -34,7 +34,8 @@
     return jnp.where(((turn + 1) & 2) == 2, -cos, cos), jnp.where((turn & 2) == 2, -sin, sin)
 
 
-def table_kernel(lats, lons, wlist_hbm, trunc_hbm, table, keep_ref, own_ref, wlist_ref, trunc_ref, small):
+def fourier_kernel(wlist_hbm, trunc_hbm, grid_hbm, out_ref, own_ref, wlist_ref, trunc_ref, grid_ref, table, rows, small, sems):
+    vectors, fields, lats, lons = grid_ref.shape
     bands = wlist_ref.shape[0]
     total_lat = lats * bands
     members = 2 * bands
@@ -42,6 +43,13 @@
     get_trunc = pltpu.make_async_copy(trunc_hbm, trunc_ref, small.at[1])
     get_wlist.start()
     get_trunc.start()
+    half = vectors // 2
+    fetches = [
+        pltpu.make_async_copy(grid_hbm.at[pl.ds(v, half)], grid_ref.at[pl.ds(v, half)], sems.at[n])
+        for n, v in enumerate(range(0, vectors, half))
+    ]
+    for fetch in fetches:
+        fetch.start()
     row = lax.broadcasted_iota(jnp.int32, (members, 128), 0)
     lane = lax.broadcasted_iota(jnp.int32, (members, 128), 1)
     get_wlist.wait()
@@ -62,22 +70,15 @@
         table[members:, 128 * i : 128 * (i + 1)] = (-(cs * fine_cos + cc * fine_sin)).astype(BF16)
     get_trunc.wait()
     keep = mvals[:, :lats] <= trunc_ref[...]
-    keep = jnp.where(keep, 1.0, 0.0)
-    keep_ref[...] = jnp.concatenate([keep, keep], axis=0)
-
-
-def pack_kernel(spectra_ref, keep_ref, out_ref, rows):
-    bands = out_ref.shape[0]
-    lats = keep_ref.shape[1]
-    fields, vectors = 2, spectra_ref.shape[1] // (2 * lats)
-    keep = keep_ref[...] > 0
+    keep = jnp.concatenate([keep, keep], axis=0)
     depth = out_ref.shape[1]
     wide = lax.broadcasted_iota(jnp.int32, (bands, 128), 1)
     for v in range(vectors):
+        if v % half == 0:
+            fetches[v // half].wait()
         fields_of = []
         for f in range(fields):
-            place = lats * (v * fields + f)
-            spectra = spectra_ref[:, place : place + lats]
+            spectra = lax.dot_general(table[...], grid_ref[v, f], NT, preferred_element_type=F32)
             spectra = jnp.where(keep, spectra, 0.0)
             fields_of.append(jnp.pad(spectra, ((0, 0), (0, 128 - lats))))
         for r in range(2):
@@ -206,34 +207,26 @@
     vectors, fields, lats, lons = grid.shape
     bands = wlist.shape[0]
     depth = 6 * vectors
-    table, keep, own = pl.pallas_call(
-        functools.partial(table_kernel, lats, lons),
-        name="table",
+    return pl.pallas_call(
+        fourier_kernel,
+        name="fourier",
         out_shape=(
-            jax.ShapeDtypeStruct((4 * bands, lons), BF16),
-            jax.ShapeDtypeStruct((4 * bands, lats), F32),
+            jax.ShapeDtypeStruct((bands, depth, 128), BF16),
             jax.ShapeDtypeStruct((8, 128), jnp.int32),
         ),
-        in_specs=[HBM, HBM],
-        out_specs=(VMEM, VMEM, VMEM),
+        in_specs=[HBM, HBM, HBM],
+        out_specs=(VMEM, VMEM),
         scratch_shapes=[
             pltpu.SMEM((bands,), jnp.int32),
             pltpu.VMEM((1, lats), jnp.int32),
+            pltpu.VMEM(grid.shape, BF16),
+            pltpu.VMEM((4 * bands, lons), BF16),
+            pltpu.VMEM((bands * depth, 128), F32),
+            pltpu.SemaphoreType.DMA((2,)),
             pltpu.SemaphoreType.DMA((2,)),
         ],
         compiler_params=PARAMS,
-    )(in_hbm(wlist), in_hbm(trunc.reshape(1, lats)))
-    spectra = lax.dot_general(table, grid.reshape(-1, lons), NT, preferred_element_type=F32)
-    lat_rows = pl.pallas_call(
-        pack_kernel,
-        name="pack",
-        out_shape=jax.ShapeDtypeStruct((bands, depth, 128), BF16),
-        in_specs=[VMEM, VMEM],
-        out_specs=VMEM,
-        scratch_shapes=[pltpu.VMEM((bands * depth, 128), F32)],
-        compiler_params=PARAMS,
-    )(spectra, keep)
-    return lat_rows, own
+    )(in_hbm(wlist), in_hbm(trunc.reshape(1, lats)), in_hbm(grid))
 
 
 def legendre(own, received, leg_even, leg_odd, vectors, tans):

time: 56.2 us -> 55.7 us (level)
  Pallas kernels: 3.19 us -> 4.59 us
  matrix products: 1.1 us -> 0 us
  local copies, waits for them, and re-layouts: 0.79 us -> 0.01 us
    pallas_call x2 -> x1, Pallas kernels: 1.49 us -> 2.9 us  [fourier(): pl.pallas_call(fourier_kernel, name='fourier', out_shape=(jax.ShapeDtypeS...]
    dot_general x1 -> x0, matrix products: 1.1 us -> none  [fourier(): lax.dot_general(table, grid.reshape(-1, lons), NT, preferred_element_type...]
    unnamed x6 -> x4, local copies, waits for them, and re-layouts: 0.79 us -> 0.01 us
where the time goes in v8:
time: 55.7 us; the launch traced here: 55.5 us
  blocking collectives  50.3 us (90%)
  Pallas kernels  4.59 us (8%)
  between operations  0.67 us (1%)
    all_to_all x1, blocking collectives, on_device(): lax.all_to_all(lat_rows, 'band', 0, 0, axis_index_groups=[FOURIER_BANDS],...  16.8 us
    all_to_all x1, blocking collectives, on_device(): lax.all_to_all(products, ('band', 'x', 'z'), 0, 0, axis_index_groups=prod...  16.8 us
    all_to_all x1, blocking collectives, on_device(): lax.all_to_all(tiles, ('x', 'z'), 0, 0, axis_index_groups=[tan_group], ti...  16.7 us
    pallas_call x1, Pallas kernels, fourier(): pl.pallas_call(fourier_kernel, name='fourier', out_shape=(jax.ShapeDtypeS...  2.9 us

profile of v8, /device:TPU:1, one launch (start us, length us, event | category | flops | bytes accessed | tf_op | source)
XLA Modules:
  0.0 55.5 jit_solution(7239838698261838980)
XLA Ops:
  0.6 0.0 copy-start.1
  0.6 0.0 copy-start
  0.7 2.9 %fourier.1 = (bf16[16,24,128]{2,1,0:T(8,128)(2,1)S(1)}, s32[8,128]{1,0:T(8,128)S(1)}) custom-call(s32[16]{0:T(128)} %wlist_hbm.1, s32[1,80]{1,0:T(1,128)} %bitcast.12, bf16[4,2,80,2560]{3,2,1,0:T(8,128)(2,1)} %grid_hbm.1), custom_call_target="tpu_custom_call" | custom-call | tf_op jit(solution)/shard_map/fourier/pallas_call | solution.py:210
  3.6 16.8 %all_to_all.15.rows_ref = bf16[16,24,128]{2,1,0:T(8,128)(2,1)S(1)} all-to-all(bf16[16,24,128]{2,1,0:T(8,128)(2,1)S(1)} %get-tuple-element.12), channel_id=1, replica_groups={{352,384,416,448,480,0,32,64,96,128,160,192,224,256,288,320},{353,385,4..., dimensions={0} | all-to-all | bytes 196608 | tf_op jit(solution)/shard_map/all_to_all | solution.py:286
  20.4 0.0 copy-done.1
  20.4 0.0 copy-done
  20.4 0.8 %legendre.1 = (bf16[16,48,128]{2,1,0:T(8,128)(2,1)S(1)}, f32[16,641]{1,0:T(8,128)S(1)}, f32[16,640]{1,0:T(8,128)S(1)}) custom-call(s32[8,128]{1,0:T(8,128)S(1)} %get-tuple-element.11.own_ref, bf16[16,24,128]{2,1,0:T(8,128)(2,1)S(1)} %all_to_all.15.rows_ref, bf16[1,641,640]{2,1,0:T(8,128)(2,1)S(1)} %bitcast.7, bf16[1,640,640]{2,1,0:T(8,128)(2,1)S(1)} %copy-done.1), custom_call_target="tpu_custom_call" | custom-call | tf_op jit(solution)/shard_map/legendre/pallas_call | solution.py:235
  21.2 16.7 %all_to_all.16 = bf16[32,12,2,128]{3,2,1,0:T(2,128)(2,1)S(1)} all-to-all(bf16[32,12,2,128]{3,2,1,0:T(2,128)(2,1)S(1)} %bitcast.11), channel_id=1, replica_groups={{22,23,14,15,30,31,6,7,16,17,20,21,8,9,12,13,24,25,28,29,0,1,4,5,18,19,..., dimensions={0} | all-to-all | bytes 393216 | tf_op jit(solution)/shard_map/all_to_all | solution.py:294
  37.9 0.2 gram.1
  38.1 16.8 %all_to_all.17 = bf16[128,4,128]{2,1,0:T(4,128)(2,1)S(1)} all-to-all(bf16[128,4,128]{2,1,0:T(4,128)(2,1)S(1)} %bitcast.10), channel_id=1, replica_groups={{368,369,352,353,360,361,376,377,80,81,64,65,72,73,88,89,112,113,96,97,..., dimensions={0} | all-to-all | bytes 262144 | tf_op jit(solution)/shard_map/all_to_all | solution.py:301
  54.9 0.7 %finish.1 = (f32[4,128]{1,0:T(4,128)}, f32[1,4,2,2,641]{4,3,2,1,0:T(2,128)}, f32[1,4,2,2,640]{4,3,2,1,0:T(2,128)}) custom-call(bf16[64,8,128]{2,1,0:T(8,128)(2,1)S(1)} %bitcast.9, f32[16,641]{1,0:T(8,128)S(1)} %get-tuple-element.14.even_in_ref, f32[16,640]{1,0:T(8,128)S(1)} %get-tuple-element.15.odd_in_ref), custom_call_target="tpu_custom_call" | custom-call | tf_op jit(solution)/shard_map/finish/pallas_call | solution.py:265
Async XLA Ops:
  0.6 19.7 %copy-start.1 = (bf16[1,640,640]{2,1,0:T(8,128)(2,1)S(1)}, bf16[1,640,640]{2,1,0:T(8,128)(2,1)}, u32[]{:S(2)}) copy-start(bf16[1,640,640]{2,1,0:T(8,128)(2,1)} %odd_ref.1) | copy-start | bytes 2457604
  0.6 19.7 %copy-start = (bf16[1,640,641]{1,2,0:T(8,128)(2,1)S(1)}, bf16[1,640,641]{1,2,0:T(8,128)(2,1)}, u32[]{:S(2)}) copy-start(bf16[1,640,641]{1,2,0:T(8,128)(2,1)} %param.8) | copy-start | bytes 2461444

commit v9 on v8

--- a/solution.py
+++ b/solution.py
@@ -71,7 +71,7 @@
     get_trunc.wait()
     keep = mvals[:, :lats] <= trunc_ref[...]
     keep = jnp.concatenate([keep, keep], axis=0)
-    depth = out_ref.shape[1]
+    depth = out_ref.shape[1] // 2
     wide = lax.broadcasted_iota(jnp.int32, (bands, 128), 1)
     for v in range(vectors):
         if v % half == 0:
@@ -81,8 +81,8 @@
             spectra = lax.dot_general(table[...], grid_ref[v, f], NT, preferred_element_type=F32)
             spectra = jnp.where(keep, spectra, 0.0)
             fields_of.append(jnp.pad(spectra, ((0, 0), (0, 128 - lats))))
+        others = jnp.zeros((bands, 128), F32)
         for r in range(2):
-            others = jnp.zeros((bands, 128), F32)
             for p in range(2):
                 start = (r * 2 + p) * bands
                 one, two = (spectra[start : start + bands] for spectra in fields_of)
@@ -90,15 +90,15 @@
                     wide < 64, one, pltpu.roll(two, 64, 1)
                 )
                 for f, spectra in enumerate((one, two)):
-                    place = 16 * (p * fields + f)
+                    place = 64 * r + 16 * (p * fields + f)
                     mine = (wide >= place) & (wide < place + 16)
                     others = jnp.where(mine, pltpu.roll(spectra, (place + 64) % 128, 1), others)
-            rows[pl.ds((4 + r) * vectors + v, bands, stride=depth), :] = others
-    out_ref[...] = rows[...].astype(BF16).reshape(out_ref.shape)
+        rows[pl.ds(4 * vectors + v, bands, stride=depth), :] = others
+    out_ref[...] = rows[...].reshape(out_ref.shape).astype(BF16)
 
 
 def legendre_kernel(own_ref, rows_ref, even_t_ref, odd_ref, send_ref, even_ref, odd_out_ref, fold):
-    bands = rows_ref.shape[0]
+    bands = 2 * rows_ref.shape[0]
     half_bands = bands // 2
     hemisphere = odd_ref.shape[1]
     lats = hemisphere // half_bands
@@ -107,8 +107,11 @@
     own = own_ref[0:1, 0:1]
 
     def slab(band):
-        packed = rows_ref[FOURIER_BANDS.index(band)].astype(F32)
-        others = packed[2 * depth // 4 :]
+        place = FOURIER_BANDS.index(band)
+        start = place % 2 * (5 * depth // 8)
+        packed = rows_ref[place // 2].astype(F32)[start : start + 5 * depth // 8]
+        others = packed[depth // 2 :]
+        others = jnp.concatenate([others, pltpu.roll(others, 64, 1)], axis=0)
         groups = []
         for p in range(2):
             for f in range(2):
@@ -206,12 +209,12 @@
 def fourier(wlist, trunc, grid):
     vectors, fields, lats, lons = grid.shape
     bands = wlist.shape[0]
-    depth = 6 * vectors
+    depth = 5 * vectors
     return pl.pallas_call(
         fourier_kernel,
         name="fourier",
         out_shape=(
-            jax.ShapeDtypeStruct((bands, depth, 128), BF16),
+            jax.ShapeDtypeStruct((bands // 2, 2 * depth, 128), BF16),
             jax.ShapeDtypeStruct((8, 128), jnp.int32),
         ),
         in_specs=[HBM, HBM, HBM],
@@ -283,9 +286,10 @@
     vectors, fields, lats, _ = grid.shape
     total_lat = lats * bands
     lat_rows, own = fourier(wlist, trunc, grid)
-    received = lax.all_to_all(
-        lat_rows, "band", 0, 0, axis_index_groups=[FOURIER_BANDS], tiled=True
-    )
+    slabs = lat_rows.shape
+    lat_rows = lat_rows.reshape(bands, 5, vectors, 128)
+    received = lax.all_to_all(lat_rows, "band", 0, 0, axis_index_groups=[FOURIER_BANDS], tiled=True)
+    received = received.reshape(slabs)
     tiles, even, odd = legendre(own, received, leg_even, leg_odd, vectors, tans)
     slab = tiles.shape
     tiles = tiles.reshape(tans, slab[1] // 4, 2, 128)

time: 55.7 us -> 55.5 us (level)
  no operation moved by 1% of the time
where the time goes in v9:
time: 55.5 us; the launch traced here: 55.3 us
  blocking collectives  49.9 us (90%)
  Pallas kernels  4.71 us (8%)
  between operations  0.67 us (1%)
    all_to_all x1, blocking collectives, on_device(): lax.all_to_all(tiles, ('x', 'z'), 0, 0, axis_index_groups=[tan_group], ti...  16.8 us
    all_to_all x1, blocking collectives, on_device(): lax.all_to_all(products, ('band', 'x', 'z'), 0, 0, axis_index_groups=prod...  16.7 us
    all_to_all x1, blocking collectives, on_device(): lax.all_to_all(lat_rows, 'band', 0, 0, axis_index_groups=[FOURIER_BANDS],...  16.4 us
    pallas_call x1, Pallas kernels, fourier(): pl.pallas_call(fourier_kernel, name='fourier', out_shape=(jax.ShapeDtypeS...  2.89 us

profile of v9, /device:TPU:1, one launch (start us, length us, event | category | flops | bytes accessed | tf_op | source)
XLA Modules:
  0.0 55.3 jit_solution(14790651448184205865)
XLA Ops:
  0.6 0.0 copy-start.1
  0.6 0.0 copy-start
  0.7 2.9 %fourier.1 = (bf16[8,40,128]{2,1,0:T(8,128)(2,1)S(1)}, s32[8,128]{1,0:T(8,128)S(1)}) custom-call(s32[16]{0:T(128)} %wlist_hbm.1, s32[1,80]{1,0:T(1,128)} %bitcast.16, bf16[4,2,80,2560]{3,2,1,0:T(8,128)(2,1)} %grid_hbm.1), custom_call_target="tpu_custom_call" | custom-call | tf_op jit(solution)/shard_map/fourier/pallas_call | solution.py:213
  3.6 16.4 %all_to_all.15 = bf16[16,5,4,128]{3,2,1,0:T(4,128)(2,1)S(1)} all-to-all(bf16[16,5,4,128]{3,2,1,0:T(4,128)(2,1)S(1)} %bitcast.15), channel_id=1, replica_groups={{352,384,416,448,480,0,32,64,96,128,160,192,224,256,288,320},{353,385,4..., dimensions={0} | all-to-all | bytes 163840 | tf_op jit(solution)/shard_map/all_to_all | solution.py:291
  20.0 0.0 copy-done.1
  20.0 0.0 copy-done
  20.0 0.9 %legendre.1 = (bf16[16,48,128]{2,1,0:T(8,128)(2,1)S(1)}, f32[16,641]{1,0:T(8,128)S(1)}, f32[16,640]{1,0:T(8,128)S(1)}) custom-call(s32[8,128]{1,0:T(8,128)S(1)} %get-tuple-element.11.own_ref, bf16[8,40,128]{2,1,0:T(8,128)(2,1)S(1)} %bitcast.13, bf16[1,641,640]{2,1,0:T(8,128)(2,1)S(1)} %bitcast.9, bf16[1,640,640]{2,1,0:T(8,128)(2,1)S(1)} %copy-done.1), custom_call_target="tpu_custom_call" | custom-call | tf_op jit(solution)/shard_map/legendre/pallas_call | solution.py:238
  20.9 16.8 %all_to_all.16 = bf16[32,12,2,128]{3,2,1,0:T(2,128)(2,1)S(1)} all-to-all(bf16[32,12,2,128]{3,2,1,0:T(2,128)(2,1)S(1)} %bitcast.14), channel_id=1, replica_groups={{22,23,14,15,30,31,6,7,16,17,20,21,8,9,12,13,24,25,28,29,0,1,4,5,18,19,..., dimensions={0} | all-to-all | bytes 393216 | tf_op jit(solution)/shard_map/all_to_all | solution.py:298
  37.7 0.2 gram.1
  38.0 16.7 %all_to_all.17 = bf16[128,4,128]{2,1,0:T(4,128)(2,1)S(1)} all-to-all(bf16[128,4,128]{2,1,0:T(4,128)(2,1)S(1)} %bitcast.12), channel_id=1, replica_groups={{368,369,352,353,360,361,376,377,80,81,64,65,72,73,88,89,112,113,96,97,..., dimensions={0} | all-to-all | bytes 262144 | tf_op jit(solution)/shard_map/all_to_all | solution.py:305
  54.6 0.7 %finish.1 = (f32[4,128]{1,0:T(4,128)}, f32[1,4,2,2,641]{4,3,2,1,0:T(2,128)}, f32[1,4,2,2,640]{4,3,2,1,0:T(2,128)}) custom-call(bf16[64,8,128]{2,1,0:T(8,128)(2,1)S(1)} %bitcast.11, f32[16,641]{1,0:T(8,128)S(1)} %get-tuple-element.14.even_in_ref, f32[16,640]{1,0:T(8,128)S(1)} %get-tuple-element.15.odd_in_ref), custom_call_target="tpu_custom_call" | custom-call | tf_op jit(solution)/shard_map/finish/pallas_call | solution.py:268
Async XLA Ops:
  0.6 19.4 %copy-start.1 = (bf16[1,640,640]{2,1,0:T(8,128)(2,1)S(1)}, bf16[1,640,640]{2,1,0:T(8,128)(2,1)}, u32[]{:S(2)}) copy-start(bf16[1,640,640]{2,1,0:T(8,128)(2,1)} %odd_ref.1) | copy-start | bytes 2457604
  0.6 19.4 %copy-start = (bf16[1,640,641]{1,2,0:T(8,128)(2,1)S(1)}, bf16[1,640,641]{1,2,0:T(8,128)(2,1)}, u32[]{:S(2)}) copy-start(bf16[1,640,641]{1,2,0:T(8,128)(2,1)} %param.8) | copy-start | bytes 2461444
